TPU v7x, 512 devices: a whole 4x8x8 slice. The times are simulated.
512 devices in a mesh: ctx: 32 (over x_lo, y, core), head: 16 (over z, x_hi).
Axes of the slice: x: 4 (x_hi: 2, x_lo: 2; x = x_hi * 2 + x_lo), y: 8, z: 8, core: 2. Of those that a mesh axis runs over, the one named last changes fastest.
Arguments:
- latent_keys: bfloat16 [4096, 576], P('ctx'), may hold values from -6 to 6
- index_keys: bfloat16 [4096, 128], P('ctx'), may hold values from -6 to 6
- main_query: bfloat16 [4096, 73728], P('ctx', 'head'), may hold values from -107 to 107
- index_query: bfloat16 [4096, 8192], P('ctx', 'head'), may hold values from -10 to 10
- index_weight: bfloat16 [4096, 64], P('ctx', 'head'), may hold values from 0.029907227 to 0.29882812
- segment_ids: int32 [4096], replicated, may hold values from 0 to 7, never falling along the last dimension, each value on 1 to 1024 neighbouring positions
- block_order: int32 [64], replicated, may hold values from 0 to 63, each once
Outputs:
- kl: float32 [4096], P('ctx')
Inputs may be any that keep to these rules, and one draw needn't show every extreme that they name: `segment_ids`: never falls along the sequence; each document holds 1 to 1024 positions and one holds exactly that many. `block_order`: each block number appears once.
All inputs are finite; a program needn't handle non-finite values.
Results may differ from a plain program's by a relative error of at most 0.0003.
Values may be sent and summed in bfloat16 or wider, within the bound.
A program may use at most 64 MiB of HBM per device.

v0:
```python
import jax
import jax.numpy as jnp
from jax import lax
from jax.sharding import PartitionSpec as P

HEADS = 128


score_scale = 192.0 ** (-0.5)
masked_fill = -1e30


def in_one_piece(arrays, axis, dim, along):
    ends, at = ([], 0)
    for a in arrays[:-1]:
        at += a.shape[along]
        ends.append(at)
    both = jnp.concatenate(arrays, axis=along)
    return tuple(jnp.split(lax.all_gather(both, axis, axis=dim, tiled=True), ends, axis=along))


def cut_along(x, dim, size):
    before, after = (x.shape[:dim], x.shape[dim + 1 :])
    return jnp.moveaxis(x.reshape(*before, size, -1, *after), dim, 0)


def sum_at_owner(x, axis, dim):
    size = lax.axis_size(axis)
    tiles = lax.all_to_all(cut_along(x, dim, size), axis, 0, 0, tiled=True)
    return jnp.sum(tiles, axis=0)


def copy_for_each(x, axis):
    size = lax.axis_size(axis)
    return lax.all_to_all(jnp.broadcast_to(x[None], (size, *x.shape)), axis, 0, 0, tiled=True)


def gathered_once(x, axis):
    leaves = jax.tree.leaves(x)
    sequence = sorted(range(len(leaves)), key=lambda k: -leaves[k].size)
    width = (1, *leaves[sequence[0]].shape)[-1]
    lines = [
        jnp.pad(leaves[k].reshape(-1), (0, -leaves[k].size % width)).reshape(-1, width)
        for k in sequence
    ]
    both, at, found = (copy_for_each(jnp.concatenate(lines), axis), 0, {})
    for k, line in zip(sequence, lines):
        slab = both[:, at : at + len(line)].reshape(len(both), -1)
        found[k] = slab[:, : leaves[k].size].reshape(-1, *leaves[k].shape)
        at += len(line)
    numbers = iter(range(len(leaves)))
    return jax.tree.map(lambda _: found[next(numbers)], x)


def folded_in_pairs(pieces, combine):
    while len(jax.tree.leaves(pieces)[0]) > 1:
        pieces = jax.vmap(combine)(
            *(jax.tree.map(lambda part: part[side::2], pieces) for side in (0, 1))
        )
    return jax.tree.map(lambda part: part[0], pieces)


def combined_all(x, axis, combine):
    pieces = gathered_once(x, axis)
    return folded_in_pairs(pieces, combine)


def key_positions(block_order, half_block):
    offsets = jnp.arange(half_block, dtype=jnp.int32)
    return (block_order[:, None] * half_block + offsets[None, :]).reshape(-1)


def visible_mask(query_pos, key_pos, segment_ids):
    query_seg = jnp.take(segment_ids, query_pos)
    key_seg = jnp.take(segment_ids, key_pos)
    return (key_pos[None, :] <= query_pos[:, None]) & (key_seg[None, :] == query_seg[:, None])


def head_scores(query_head, key_table):
    raw = lax.dot_general(
        query_head, key_table, (((1,), (1,)), ((), ())), preferred_element_type=jnp.float32
    )
    return raw * score_scale


def softmax_add(running, scores, visible):
    masked = jnp.where(visible, scores, masked_fill)
    row_max = jnp.max(masked, axis=1, keepdims=True)
    powers = jnp.where(visible, jnp.exp(masked - row_max), 0.0)
    return running + powers / jnp.sum(powers, axis=1, keepdims=True)


def index_scores(query_rows, gains, key_table):
    row_count = query_rows.shape[0]
    head_count = gains.shape[1]
    head_width = query_rows.shape[1] // head_count
    stacked = jnp.moveaxis(query_rows.reshape(row_count, head_count, head_width), 1, 0)
    gain_rows = jnp.moveaxis(gains.astype(jnp.float32), 1, 0)

    def add_head(running, pieces):
        query_head, gain_head = pieces
        dots = lax.dot_general(
            query_head, key_table, (((1,), (1,)), ((), ())), preferred_element_type=jnp.float32
        )
        return (running + gain_head[:, None] * jnp.maximum(dots, 0.0), None)

    start_sum = jnp.zeros((row_count, key_table.shape[0]), jnp.float32)
    running, _ = lax.scan(add_head, start_sum, (stacked, gain_rows))
    return running


def row_terms(target, index_score, visible):
    masked = jnp.where(visible, index_score, masked_fill)
    row_max = jnp.max(masked, axis=1)
    exp_sum = jnp.sum(jnp.where(visible, jnp.exp(masked - row_max[:, None]), 0.0), axis=1)
    positive = target > 0.0
    safe_target = jnp.where(positive, target, 1.0)
    entropy_sum = jnp.sum(jnp.where(positive, target * jnp.log(safe_target), 0.0), axis=1)
    cross_sum = jnp.sum(jnp.where(visible, target * index_score, 0.0), axis=1)
    target_sum = jnp.sum(target, axis=1)
    return (row_max, exp_sum, entropy_sum, cross_sum, target_sum)


def combine_rows(first, second):
    row_max = jnp.maximum(first[0], second[0])
    exp_sum = first[1] * jnp.exp(first[0] - row_max) + second[1] * jnp.exp(second[0] - row_max)
    return (row_max, exp_sum, first[2] + second[2], first[3] + second[3], first[4] + second[4])


def finish_rows(row_max, exp_sum, entropy_sum, cross_sum, target_sum):
    return entropy_sum - cross_sum + (row_max + jnp.log(exp_sum)) * target_sum


def per_device(
    latent_keys, index_keys, main_query, index_query, index_weight, segment_ids, block_order
):
    row_count = latent_keys.shape[0]
    half_block = row_count // 2
    all_latent, all_index = in_one_piece((latent_keys, index_keys), "ctx", 0, 1)
    key_width = all_latent.shape[1]
    key_pos = key_positions(block_order, half_block)
    query_pos = lax.dynamic_slice_in_dim(key_pos, lax.axis_index("ctx") * row_count, row_count)
    heads_here = main_query.shape[1] // key_width
    stacked = jnp.moveaxis(main_query.reshape(row_count, heads_here, key_width), 1, 0)
    ctx_count = lax.axis_size("ctx")
    reach = ctx_count // 2 + 2
    slot_count = 2 * ctx_count
    slot_ids = jnp.arange(slot_count, dtype=jnp.int32)
    slot_of = jnp.sum(
        slot_ids[None, :] * (block_order[None, :] == slot_ids[:, None]).astype(jnp.int32), axis=1
    )
    mine = lax.dynamic_slice_in_dim(block_order, lax.axis_index("ctx") * 2, 2)
    wanted = mine[:, None] - (reach - 1) + jnp.arange(reach, dtype=jnp.int32)[None, :]
    valid_block = wanted >= 0
    safe_block = jnp.maximum(wanted, 0)
    stored_slot = jnp.take(slot_of, safe_block)
    offsets = jnp.arange(half_block, dtype=jnp.int32)
    window_rows = (stored_slot[:, :, None] * half_block + offsets[None, None, :]).reshape(-1)
    window_pos = (safe_block[:, :, None] * half_block + offsets[None, None, :]).reshape(-1)
    window_valid = jnp.broadcast_to(valid_block[:, :, None], (2, reach, half_block)).reshape(-1)
    window_owner = jnp.broadcast_to(
        jnp.arange(2, dtype=jnp.int32)[:, None, None], (2, reach, half_block)
    ).reshape(-1)
    row_block = jnp.arange(row_count, dtype=jnp.int32) // half_block
    window_visible = visible_mask(query_pos, window_pos, segment_ids)
    window_visible = (
        window_visible & window_valid[None, :] & (window_owner[None, :] == row_block[:, None])
    )
    window_latent = jnp.take(all_latent, window_rows, axis=0)
    window_index = jnp.take(all_index, window_rows, axis=0)
    window_len = window_rows.shape[0]

    def add_window(running, query_head):
        return (softmax_add(running, head_scores(query_head, window_latent), window_visible), None)

    partial_value, _ = lax.scan(
        add_window, jnp.zeros((row_count, window_len), jnp.float32), stacked
    )
    share_len = window_len // lax.axis_size("head")
    share_start = lax.axis_index("head") * share_len
    query_rows, gains = (
        lax.all_gather(index_query, "head", axis=1, tiled=True),
        lax.all_gather(index_weight, "head", axis=1, tiled=True),
    )
    share_keys = lax.dynamic_slice_in_dim(window_index, share_start, share_len, 0)
    index_score = index_scores(query_rows, gains, share_keys)
    target = sum_at_owner(partial_value, "head", 1) / HEADS
    share_visible = lax.dynamic_slice_in_dim(window_visible, share_start, share_len, 1)
    local_terms = row_terms(target, index_score, share_visible)
    row_max, exp_sum, entropy_sum, cross_sum, target_sum = combined_all(
        local_terms, "head", combine_rows
    )
    return finish_rows(row_max, exp_sum, entropy_sum, cross_sum, target_sum)


def solution(mesh):
    in_specs = (
        P("ctx", None),
        P("ctx", None),
        P("ctx", "head"),
        P("ctx", "head"),
        P("ctx", "head"),
        P(),
        P(),
    )
    out_specs = P("ctx")
    return jax.shard_map(
        per_device, mesh=mesh, in_specs=in_specs, out_specs=out_specs, check_vma=False
    )
```

profile of v0, /device:TPU:24, one launch (start us, length us, event | category | flops | bytes accessed | tf_op | source)
XLA Modules:
  0.0 281.9 jit_solution(2342039676385836117)
XLA Ops:
  6.5 1.1 copy.26
  7.6 1.5 pad_maximum_fusion
  9.2 1.7 copy.25
  12.8 47.0 %all-gather = bf16[16,4,128]{2,1,0:T(4,128)(2,1)S(1)} all-gather(bf16[1,4,128]{2,1,0:T(4,128)(2,1)S(1)} %bitcast.78), channel_id=1, replica_groups=mesh['ctx'=32,'head'=16] {'head'}, dimensions={0}, use_global_device_ids=true | all-gather | bytes 17408 | tf_op jit(solution)/shard_map/all_gather | solution.py:183
  60.7 1.1 gather_fusion.1
  61.9 12.3 %gather_fusion = s32[2304]{0:T(1024)S(1)} fusion(s32[4096]{0:T(1024)S(1)} %copy-done, s32[3072]{0:T(1024)S(1)} %pad_clamp_fusion.1), kind=kCustom, calls=%fused_computation | custom fusion | bytes 27648 | tf_op jit(solution)/shard_map/jit(_take)/gather | solution.py:75
  74.4 1.4 copy.28
  75.8 9.7 %all-gather.6.cloned.1.call-done = bf16[4096,704]{1,0:T(8,128)(2,1)} async-done(((bf16[128,704]{1,0:T(8,128)(2,1)}), bf16[4096,704]{1,0:T(8,128)(2,1)}) %all-gather.6.cloned.1.call-update) | async-done | bytes 5767184 | tf_op jit(solution)/shard_map/all_gather | solution.py:19
  85.4 5.3 %split.9 = bf16[4096,576]{1,0:T(8,128)(2,1)} slice(bf16[4096,704]{1,0:T(8,128)(2,1)} %all-gather.6.cloned.1.call-done), slice={[0:4096], [0:576]} | slice | bytes 9437184 | tf_op jit(solution)/shard_map/split | solution.py:19
  90.8 11.4 %gather_fusion.4 = bf16[2304,576]{1,0:T(8,128)(2,1)} fusion(bf16[4096,576]{1,0:T(8,128)(2,1)} %split.9, s32[3072]{0:T(1024)S(1)} %pad_clamp_fusion), kind=kCustom, calls=%fused_computation.4 | custom fusion | bytes 5317632 | tf_op jit(solution)/shard_map/jit(_take)/gather | solution.py:169
  102.2 3.8 %broadcast_select_fusion = bf16[2304,576]{1,0:T(8,128)(2,1)} fusion(bf16[2304,576]{1,0:T(8,128)(2,1)} %gather_fusion.4, pred[2304]{0:T(1024)(128)(4,1)S(1)} %compare_and_fusion.2), kind=kLoop, calls=%fused_computation.22 | loop fusion | flops 1327104 | bytes 5310720 | tf_op jit(solution)/shard_map/jit(_take)/select_n | solution.py:169
  105.9 37.4 %while.23 = (s32[]{:T(128)}, f32[128,2304]{1,0:T(8,128)S(1)}, bf16[8,128,576]{1,2,0:T(8,128)(2,1)}, bf16[2304,576]{1,0:T(8,128)(2,1)}, s32[128]{0:T(128)S(1)}, /...) while((s32[]{:T(128)}, f32[128,2304]{1,0:T(8,128)S(1)}, ...), condition=%wide.region_8.9_spmd.clone, body=%wide.region_5.8_spmd.clone.sunk | while | flops 348290816 | bytes 9091987 | solution.py:176
  105.9 3.1 %fusion.38 = (f32[128]{0:T(128)S(1)}, f32[128,2304]{1,0:T(8,128)S(1)}) fusion(bf16[2304,576]{1,0:T(8,128)(2,1)} %get-tuple-element.379, bf16[8,128,576]{1,2,0:T(8,128)(2,1)} %get-tuple-element.378, s32[]{:T(128)S(6)} %copy.49, s32[128]{0:T(128)S(1)} %get-tuple-element.385, s32[2304]{0:T(1024)S(1)} %get-tuple-element.386, ...), kind=kOutput, calls=%fused_computation.75.clone.1 | convolution fusion | flops 342392704 | bytes 4308228 | tf_op jit(solution)/shard_map/while/body/eval_jaxpr/dot_general | solution.py:80
  110.6 3.1 %fusion.38 = (f32[128]{0:T(128)S(1)}, f32[128,2304]{1,0:T(8,128)S(1)}) fusion(bf16[2304,576]{1,0:T(8,128)(2,1)} %get-tuple-element.379, bf16[8,128,576]{1,2,0:T(8,128)(2,1)} %get-tuple-element.378, s32[]{:T(128)S(6)} %copy.49, s32[128]{0:T(128)S(1)} %get-tuple-element.385, s32[2304]{0:T(1024)S(1)} %get-tuple-element.386, ...), kind=kOutput, calls=%fused_computation.75.clone.1 | convolution fusion | flops 342392704 | bytes 4308228 | tf_op jit(solution)/shard_map/while/body/eval_jaxpr/dot_general | solution.py:80
  115.3 3.1 %fusion.38 = (f32[128]{0:T(128)S(1)}, f32[128,2304]{1,0:T(8,128)S(1)}) fusion(bf16[2304,576]{1,0:T(8,128)(2,1)} %get-tuple-element.379, bf16[8,128,576]{1,2,0:T(8,128)(2,1)} %get-tuple-element.378, s32[]{:T(128)S(6)} %copy.49, s32[128]{0:T(128)S(1)} %get-tuple-element.385, s32[2304]{0:T(1024)S(1)} %get-tuple-element.386, ...), kind=kOutput, calls=%fused_computation.75.clone.1 | convolution fusion | flops 342392704 | bytes 4308228 | tf_op jit(solution)/shard_map/while/body/eval_jaxpr/dot_general | solution.py:80
  119.9 3.1 %fusion.38 = (f32[128]{0:T(128)S(1)}, f32[128,2304]{1,0:T(8,128)S(1)}) fusion(bf16[2304,576]{1,0:T(8,128)(2,1)} %get-tuple-element.379, bf16[8,128,576]{1,2,0:T(8,128)(2,1)} %get-tuple-element.378, s32[]{:T(128)S(6)} %copy.49, s32[128]{0:T(128)S(1)} %get-tuple-element.385, s32[2304]{0:T(1024)S(1)} %get-tuple-element.386, ...), kind=kOutput, calls=%fused_computation.75.clone.1 | convolution fusion | flops 342392704 | bytes 4308228 | tf_op jit(solution)/shard_map/while/body/eval_jaxpr/dot_general | solution.py:80
  124.6 3.1 %fusion.38 = (f32[128]{0:T(128)S(1)}, f32[128,2304]{1,0:T(8,128)S(1)}) fusion(bf16[2304,576]{1,0:T(8,128)(2,1)} %get-tuple-element.379, bf16[8,128,576]{1,2,0:T(8,128)(2,1)} %get-tuple-element.378, s32[]{:T(128)S(6)} %copy.49, s32[128]{0:T(128)S(1)} %get-tuple-element.385, s32[2304]{0:T(1024)S(1)} %get-tuple-element.386, ...), kind=kOutput, calls=%fused_computation.75.clone.1 | convolution fusion | flops 342392704 | bytes 4308228 | tf_op jit(solution)/shard_map/while/body/eval_jaxpr/dot_general | solution.py:80
  129.3 3.1 %fusion.38 = (f32[128]{0:T(128)S(1)}, f32[128,2304]{1,0:T(8,128)S(1)}) fusion(bf16[2304,576]{1,0:T(8,128)(2,1)} %get-tuple-element.379, bf16[8,128,576]{1,2,0:T(8,128)(2,1)} %get-tuple-element.378, s32[]{:T(128)S(6)} %copy.49, s32[128]{0:T(128)S(1)} %get-tuple-element.385, s32[2304]{0:T(1024)S(1)} %get-tuple-element.386, ...), kind=kOutput, calls=%fused_computation.75.clone.1 | convolution fusion | flops 342392704 | bytes 4308228 | tf_op jit(solution)/shard_map/while/body/eval_jaxpr/dot_general | solution.py:80
  134.0 3.1 %fusion.38 = (f32[128]{0:T(128)S(1)}, f32[128,2304]{1,0:T(8,128)S(1)}) fusion(bf16[2304,576]{1,0:T(8,128)(2,1)} %get-tuple-element.379, bf16[8,128,576]{1,2,0:T(8,128)(2,1)} %get-tuple-element.378, s32[]{:T(128)S(6)} %copy.49, s32[128]{0:T(128)S(1)} %get-tuple-element.385, s32[2304]{0:T(1024)S(1)} %get-tuple-element.386, ...), kind=kOutput, calls=%fused_computation.75.clone.1 | convolution fusion | flops 342392704 | bytes 4308228 | tf_op jit(solution)/shard_map/while/body/eval_jaxpr/dot_general | solution.py:80
  138.6 3.1 %fusion.38 = (f32[128]{0:T(128)S(1)}, f32[128,2304]{1,0:T(8,128)S(1)}) fusion(bf16[2304,576]{1,0:T(8,128)(2,1)} %get-tuple-element.379, bf16[8,128,576]{1,2,0:T(8,128)(2,1)} %get-tuple-element.378, s32[]{:T(128)S(6)} %copy.49, s32[128]{0:T(128)S(1)} %get-tuple-element.385, s32[2304]{0:T(1024)S(1)} %get-tuple-element.386, ...), kind=kOutput, calls=%fused_computation.75.clone.1 | convolution fusion | flops 342392704 | bytes 4308228 | tf_op jit(solution)/shard_map/while/body/eval_jaxpr/dot_general | solution.py:80
  143.3 2.0 split.8
  145.3 4.7 %gather_fusion.3 = bf16[2304,128]{1,0:T(8,128)(2,1)S(1)} fusion(bf16[4096,128]{1,0:T(8,128)(2,1)S(1)} %split.8, s32[3072]{0:T(1024)S(1)} %pad_clamp_fusion), kind=kCustom, calls=%fused_computation.3 | custom fusion | bytes 1188864 | tf_op jit(solution)/shard_map/jit(_take)/gather | solution.py:170
  150.0 1.4 copy.30
  151.3 9.8 %all-to-all-start = ((f32[16,128,144]{1,2,0:T(8,128)}), f32[16,128,144]{1,2,0:T(8,128)S(1)}, u32[]{:S(2)}, u32[]{:S(2)}) async-start(f32[16,128,144]{1,2,0:T(8,128)} %bitcast.10), calls=%async_computation | async-start | bytes 2359296 | tf_op jit(solution)/shard_map/all_to_all | solution.py:29
  161.3 34.7 %all-gather.4.cloned.1.call-done = bf16[128,8192]{0,1:T(8,128)(2,1)} async-done(((bf16[128,512]{0,1:T(8,128)(2,1)}), bf16[128,8192]{0,1:T(8,128)(2,1)}) %all-gather.4.cloned.1.call-update) | async-done | bytes 2097168 | tf_op jit(solution)/shard_map/all_gather | solution.py:182
  195.9 61.9 %while.22 = (s32[]{:T(128)}, f32[128,144]{0,1:T(8,128)S(1)}, f32[64,128]{1,0:T(8,128)S(1)}, bf16[64,128,128]{1,2,0:T(8,128)(2,1)}, bf16[144,128]{1,0:T(8,128)(2,1)S(1)}, /*index=5*/s32[]{:T(128)}, s32[]{:T(128)}) while((s32[]{:T(128)}, f32[128,144]{0,1:T(8,128)S(1)}, f32[64,128]{1,0:T(8,128)S(1)}, bf16[64,128,128]{1,2,0:T(8,128)(2,1)}, ...), condition=%wide.region_2.3_spmd.clone, body=%wide.region_1.2_spmd.clone.sunk | while | flops 4792323 | bytes 218727 | solution.py:108
  197.9 0.9 fusion.36
  198.8 0.9 fusion.36
  199.8 0.9 fusion.36
  200.8 0.9 fusion.36
  201.7 0.9 fusion.36
  202.7 0.9 fusion.36
  203.7 0.9 fusion.36
  204.6 0.9 fusion.36
  205.6 0.9 fusion.36
  209.5 0.9 fusion.36
  210.5 0.9 fusion.36
  211.4 0.9 fusion.36
  212.4 0.9 fusion.36
  213.4 0.9 fusion.36
  214.3 0.9 fusion.36
  215.3 0.9 fusion.36
  216.3 0.9 fusion.36
  217.2 0.9 fusion.36
  218.2 0.9 fusion.36
  219.2 0.9 fusion.36
  220.1 0.9 fusion.36
  258.3 15.5 %all_to_all.10 = f32[16,5,128]{2,1,0:T(8,128)S(1)} all-to-all(f32[16,5,128]{2,1,0:T(8,128)S(1)} %broadcast_in_dim.110), channel_id=1, replica_groups=mesh['ctx'=32,'head'=16] {'head'}, dimensions={0} | all-to-all | bytes 81920 | tf_op jit(solution)/shard_map/all_to_all | solution.py:35
  (225 shorter events, 57.6 us)
Async XLA Ops:
  6.5 54.2 %copy-start = (s32[4096]{0:T(1024)S(1)}, s32[4096]{0:T(1024)}, u32[]{:S(2)}) copy-start(s32[4096]{0:T(1024)} %param.16) | copy-start | bytes 49156
  6.5 4.4 %copy-start.3 = (s32[64]{0:T(128)S(1)}, s32[64]{0:T(128)}, u32[]{:S(2)}) copy-start(s32[64]{0:T(128)} %param.17) | copy-start | bytes 772
  6.5 78.9 %all-gather.6.cloned.1.call-start = ((), (), s32[]{:S(2)}) async-start(), calls=%async_computation.3 | async-start | bytes 6488064 | tf_op jit(solution)/shard_map/all_gather | solution.py:19
  7.6 5.2 %copy-start.2 = (bf16[128,4]{0,1:T(4,128)(2,1)S(1)}, bf16[128,4]{0,1:T(4,128)(2,1)}, u32[]{:S(2)}) copy-start(bf16[128,4]{0,1:T(4,128)(2,1)} %param.15) | copy-start | bytes 3076
  9.2 186.7 %all-gather.4.cloned.1.call-start = ((), (), s32[]{:S(2)}) async-start(), calls=%async_computation.2 | async-start | bytes 2228224 | tf_op jit(solution)/shard_map/all_gather | solution.py:182
  61.9 12.5 %copy-start.1 = (bf16[128,4608]{1,0:T(8,128)(2,1)S(1)}, bf16[128,4608]{1,0:T(8,128)(2,1)}, u32[]{:S(2)}) copy-start(bf16[128,4608]{1,0:T(8,128)(2,1)} %param.13) | copy-start | bytes 3538948
  151.3 106.7 %all-to-all-start = ((f32[16,128,144]{1,2,0:T(8,128)}), f32[16,128,144]{1,2,0:T(8,128)S(1)}, u32[]{:S(2)}, u32[]{:S(2)}) async-start(f32[16,128,144]{1,2,0:T(8,128)} %bitcast.10), calls=%async_computation | async-start | bytes 2359296 | tf_op jit(solution)/shard_map/all_to_all | solution.py:29
Sparse Core Ops, SparseCore 0:
  9.5 75.8 all-gather.5
  88.6 107.2 all-gather.3
where the time goes:
time: 287 us; the launch traced here: 282 us
  matrix products  83.7 us (29%)
  blocking collectives  62.5 us (22%)
  local copies, waits for them, and re-layouts  45.6 us (16%)
  waiting for transfers between devices  44.4 us (15%)
  other arithmetic  19.9 us (7%)
  between operations  13.6 us (5%)
  starting transfers between devices  9.86 us (3%)
    dot_general x64, matrix products, add_head(): lax.dot_general(query_head, key_table, (((1,), (1,)), ((), ())), preferre...  59.2 us
    all_gather x1, blocking collectives, per_device(): lax.all_gather(index_weight, 'head', axis=1, tiled=True)  47 us
    all_gather x1, waiting for transfers between devices, per_device(): lax.all_gather(index_query, 'head', axis=1, tiled=True)  34.7 us
    dot_general x8, matrix products, head_scores(): lax.dot_general(query_head, key_table, (((1,), (1,)), ((), ())), preferre...  24.5 us
    all_to_all x1, blocking collectives, copy_for_each(): lax.all_to_all(jnp.broadcast_to(x[None], (size, *x.shape)), axis, 0, 0, t...  15.5 us
    gather x1, local copies, waits for them, and re-layouts, visible_mask(): key_seg = jnp.take(segment_ids, key_pos)  12.3 us
    gather x1, local copies, waits for them, and re-layouts, per_device(): window_latent = jnp.take(all_latent, window_rows, axis=0)  11.4 us
    all_to_all x1, starting transfers between devices, sum_at_owner(): tiles = lax.all_to_all(cut_along(x, dim, size), axis, 0, 0, tiled=True)  9.82 us
  transfers between devices with their start and end apart: 3, of which 2 were waited for; matrix products, arithmetic and copies ran while one was open for 51% of the time, Pallas kernels for 0%

commit v1 on v0

v1 whole, which is shorter than its diff:
```python
import functools
import math

import jax
import jax.numpy as jnp
from jax import lax
from jax.experimental import pallas as pl
from jax.experimental.pallas import tpu as pltpu
from jax.sharding import PartitionSpec as P

HEADS = 128
HALF = 64
FILL = -1e30
EXP_SCALE = 192.0 ** (-0.5) * math.log2(math.e)
MESH = pl.DeviceIdType.MESH
NT = (((1,), (1,)), ((), ()))
F32 = jnp.float32


def dot_nt(a, b):
    return lax.dot_general(a, b, NT, preferred_element_type=F32)


def fused(
    ny, nh, reach, share, heads, iheads,
    slots_ref, lat_in, idx_in, mq_ref, iq_ref, gain_ref, info_ref,
    out_ref,
    lat, idx, mq, iq, win, iwin, score, total, iscore, trecv, irecv, stats, srecv,
    snd, rcv, xsend, xrecv,
):
    kdim = lat_in.shape[1]
    rows_w = nh * share
    me_c, me_h = lax.axis_index("ctx"), lax.axis_index("head")
    core = me_c % 2
    y = (me_c // 2) % ny
    xl = me_c // (2 * ny)
    xh = me_h % 2
    far = ny // 2

    def ctx_of(xl_, y_, core_):
        return (xl_ * ny + y_) * 2 + core_

    up = (ctx_of(xl, (y + 1) % ny, core), me_h)
    down = (ctx_of(xl, (y + ny - 1) % ny, core), me_h)
    cross = (
        (ctx_of(1 - xl, y, core), me_h),
        (ctx_of(1 - xl, y, core), me_h - xh + (1 - xh)),
    )
    sibling = (ctx_of(xl, y, 1 - core), me_h)

    barrier = pltpu.get_barrier_semaphore()
    for dev in (up, down, cross[0], cross[1], sibling):
        pl.semaphore_signal(barrier, inc=1, device_id=dev, device_id_type=MESH)

    def greet(i, _):
        pl.semaphore_signal(
            barrier, inc=1, device_id=(me_c, (me_h + i) % nh), device_id_type=MESH
        )
        return 0

    lax.fori_loop(1, nh, greet, 0)

    own = ctx_of(xl, y, core)
    for h in (0, 1):
        idx[own * 2 + h] = idx_in[h * HALF:(h + 1) * HALF, :]
        lat[own * 2 + h] = lat_in[h * HALF:(h + 1) * HALF, :]

    pl.semaphore_wait(barrier, 5 + nh - 1)

    bufs = (idx, lat)
    started = []

    def send(b, slot, dev, lane):
        copy = pltpu.make_async_remote_copy(
            src_ref=bufs[b].at[slot], dst_ref=bufs[b].at[slot],
            send_sem=snd.at[b, lane], recv_sem=rcv.at[b, slot],
            device_id=dev, device_id_type=MESH,
        )
        copy.start()
        started.append(copy)

    def await_slot(b, slot):
        pltpu.make_async_remote_copy(
            src_ref=bufs[b].at[slot], dst_ref=bufs[b].at[slot],
            send_sem=snd.at[b, 0], recv_sem=rcv.at[b, slot],
            device_id=sibling, device_id_type=MESH,
        ).wait_recv()

    lanes = [0, 0]

    def lane(b):
        lanes[b] += 1
        return lanes[b] - 1

    def goes(dist, h, way):
        return dist < far or (dist == far and h == way)

    def ring_step(b, s):
        for h in (0, 1):
            for way in (0, 1):
                if s == 0 and way == 1:
                    continue
                if s > 0 and not goes(s, h, way):
                    continue
                yy = (y + ny - s) % ny if way == 0 else (y + s) % ny
                slot = ctx_of(xl, yy, core) * 2 + h
                if s > 0:
                    await_slot(b, slot)
                for w in ((0, 1) if s == 0 else (way,)):
                    if goes(s + 1, h, w):
                        send(b, slot, up if w == 0 else down, lane(b))
                send(b, slot, cross[h], lane(b))
                send(b, slot, sibling, lane(b))

    def cross_step(b, s):
        for h in (0, 1):
            for way in (0, 1):
                if s == 0 and way == 1:
                    continue
                if s > 0 and not goes(s, h, way):
                    continue
                yy = (y + ny - s) % ny if way == 0 else (y + s) % ny
                slot = ctx_of(1 - xl, yy, core) * 2 + h
                await_slot(b, slot)
                send(b, slot, sibling, lane(b))

    def sibling_wait(b):
        for xx in (0, 1):
            for yy in range(ny):
                for h in (0, 1):
                    await_slot(b, ctx_of(xx, yy, 1 - core) * 2 + h)

    def prepare():
        for qb in (0, 1):
            rows = slice(qb * HALF, (qb + 1) * HALF)
            for h in range(heads):
                mq[qb, h * HALF:(h + 1) * HALF, :] = mq_ref[rows, h * kdim:(h + 1) * kdim]
            for h in range(iheads):
                iq[qb, h * HALF:(h + 1) * HALF, :] = iq_ref[rows, h * 128:(h + 1) * 128]
        pad = rows_w - reach * HALF
        if pad:
            for qb in (0, 1):
                win[qb, reach * HALF:, :] = jnp.zeros((pad, kdim), jnp.bfloat16)
                iwin[qb, reach * HALF:, :] = jnp.zeros((pad, 128), jnp.bfloat16)

    def seen(which, first, count):
        kp = info_ref[which, 2:3, :] + first + lax.broadcasted_iota(jnp.int32, (count, 128), 0)
        return (kp >= info_ref[which, 0:1, :]) & (kp <= info_ref[which, 1:2, :])

    groups = 4
    size = rows_w // groups

    def left_of(count):
        return lax.broadcasted_iota(jnp.int32, (count, 128), 1) < HALF

    def part(g):
        return pl.ds(pl.multiple_of(g * size, 16), size)

    def fill(dst, src, qb):
        def body(j, _):
            at = pl.ds(pl.multiple_of(j * HALF, HALF), HALF)
            dst[qb, at, :] = src[slots_ref[qb * reach + j]]
            return 0
        lax.fori_loop(0, reach, body, 0)

    def chunk(d):
        return pl.ds(pl.multiple_of(d * share, 8), share)

    def fold(x):
        part = x[:, 0:128]
        for i in range(1, x.shape[1] // 128):
            part = part + x[:, i * 128:(i + 1) * 128]
        return part + pltpu.roll(part, HALF, 1)

    def exchange(kind, src, dst, i, start):
        to = (me_h + i) % nh
        frm = (me_h + nh - i) % nh
        there = src.at[chunk(to), :] if kind < 2 else src
        copy = pltpu.make_async_remote_copy(
            src_ref=there, dst_ref=dst.at[me_h] if start else dst.at[frm],
            send_sem=xsend.at[kind, to],
            recv_sem=xrecv.at[kind, me_h] if start else xrecv.at[kind, frm],
            device_id=(me_c, to), device_id_type=MESH,
        )
        if start:
            copy.start()
        else:
            copy.wait()
        return 0

    def index_part():
        for qb in (0, 1):
            fill(iwin, idx, qb)

        def body(d, _):
            pair = []
            for qb in (0, 1):
                dots = dot_nt(iwin[qb, part(d), :], iq[qb])
                pair.append(fold(jnp.maximum(dots, 0.0) * gain_ref[qb:qb + 1, :]))
            iscore[part(d), :] = jnp.where(left_of(size), pair[0], pair[1])
            return 0

        lax.fori_loop(0, groups, body, 0)
        lax.fori_loop(1, nh, lambda i, _: exchange(0, iscore, irecv, i, True), 0)

    def main_part():
        wide = heads * HALF
        inverses, tops = [], []
        for qb in (0, 1):
            fill(win, lat, qb)

            def first(g, top, qb=qb):
                at = part(g)
                s = dot_nt(win[qb, at, :], mq[qb])
                bias = jnp.where(seen(qb, g * size, size), 0.0, FILL)
                s = s + jnp.concatenate([bias] * (wide // 128), axis=1)
                score[qb, at, :] = s
                return jnp.maximum(top, jnp.max(s.reshape(size // 8, 8, wide), axis=0))

            top = lax.fori_loop(0, groups, first, jnp.full((8, wide), FILL, F32))
            top = jnp.max(top, axis=0, keepdims=True)

            def second(g, acc, qb=qb, top=top):
                p = jnp.exp2((score[qb, chunk(g), :] - top) * EXP_SCALE)
                score[qb, chunk(g), :] = p
                return acc + jnp.sum(p.reshape(share // 8, 8, wide), axis=0)

            acc = lax.fori_loop(0, nh, second, jnp.zeros((8, wide), F32))
            inverses.append(1.0 / jnp.sum(acc, axis=0, keepdims=True))

        def third(i, _):
            d = (me_h + i) % nh
            pair = [fold(score[qb, chunk(d), :] * inverses[qb]) for qb in (0, 1)]
            total[chunk(d), :] = jnp.where(left_of(share), pair[0], pair[1])

            @pl.when(i < nh)
            def _():
                exchange(1, total, trecv, i, True)

            return 0

        lax.fori_loop(1, nh + 1, third, 0)

    def gathered_sum(kind, src, dst):
        def body(i, acc):
            exchange(kind, src, dst, i, False)
            return acc + dst[(me_h + nh - i) % nh]
        return lax.fori_loop(1, nh, body, src[chunk(me_h), :])

    ring_step(0, 0)
    ring_step(1, 0)
    prepare()
    for s in range(1, far + 1):
        ring_step(0, s)
        cross_step(0, s - 1)
        if s % 2 == 0:
            ring_step(1, s // 2)
            cross_step(1, s // 2 - 1)
    cross_step(0, far)
    done = far // 2
    for s in range(done + 1, far):
        ring_step(1, s)
        cross_step(1, s - 1)
    sibling_wait(0)
    index_part()
    for s in range(max(far, done + 1), far + 1):
        ring_step(1, s)
        cross_step(1, s - 1)
    cross_step(1, far)
    sibling_wait(1)
    main_part()

    vis = seen(2, me_h * share, share)
    index_score = gathered_sum(0, iscore, irecv)
    masked = jnp.where(vis, index_score, FILL)
    top = jnp.max(masked, axis=0, keepdims=True)
    exp_sum = jnp.sum(jnp.where(vis, jnp.exp(masked - top), 0.0), axis=0, keepdims=True)
    target = gathered_sum(1, total, trecv) * (1.0 / HEADS)
    positive = target > 0.0
    logs = jnp.log(jnp.where(positive, target, 1.0))
    gain = jnp.sum(
        jnp.where(positive, target * logs, 0.0) - jnp.where(vis, target * index_score, 0.0),
        axis=0, keepdims=True,
    )
    mass = jnp.sum(target, axis=0, keepdims=True)
    stats[0:1, :] = top
    stats[1:2, :] = exp_sum
    stats[2:3, :] = gain
    stats[3:4, :] = mass
    stats[4:8, :] = jnp.zeros((4, 128), F32)
    lax.fori_loop(1, nh, lambda i, _: exchange(2, stats, srecv, i, True), 0)
    srecv[me_h] = stats[...]
    lax.fori_loop(1, nh, lambda i, _: exchange(2, stats, srecv, i, False), 0)
    every = srecv[...]
    tops = every[:, 0:1, :]
    peak = jnp.max(tops, axis=0, keepdims=True)
    exp_all = jnp.sum(every[:, 1:2, :] * jnp.exp(tops - peak), axis=0)
    gain_all = jnp.sum(every[:, 2:3, :], axis=0)
    mass_all = jnp.sum(every[:, 3:4, :], axis=0)
    out_ref[...] = gain_all + (peak[0] + jnp.log(exp_all)) * mass_all
    for copy in started:
        copy.wait_send()


def per_device(
    latent_keys, index_keys, main_query, index_query, index_weight, segment_ids, block_order
):
    rows, kdim = latent_keys.shape
    nc, nh = lax.axis_size("ctx"), lax.axis_size("head")
    ny = nc // 4
    blocks = 2 * nc
    reach = nc // 2 + 1
    heads = main_query.shape[1] // kdim
    iheads = index_weight.shape[1]
    share = -(-reach * HALF // (8 * nh)) * 8
    ids = jnp.arange(blocks, dtype=jnp.int32)
    mine = lax.dynamic_slice_in_dim(block_order, lax.axis_index("ctx") * 2, 2)
    wanted = jnp.maximum(
        mine[:, None] - (reach - 1) + jnp.arange(reach, dtype=jnp.int32)[None, :], 0
    ).reshape(-1)
    slots = jnp.sum(
        jnp.where(block_order[None, :] == wanted[:, None], ids[None, :], 0), axis=1
    )
    pos = (mine[:, None] * HALF + jnp.arange(HALF, dtype=jnp.int32)[None, :]).reshape(-1)
    seg = jnp.take(segment_ids, pos)
    start = jnp.sum((segment_ids[None, :] < seg[:, None]).astype(jnp.int32), axis=1)
    base = jnp.repeat(mine - (reach - 1), HALF) * HALF
    info = jnp.stack([start, pos, base])
    info = jnp.pad(info, ((0, 5), (0, 0)))
    a, b = info[:, :HALF], info[:, HALF:]
    info = jnp.stack(
        [jnp.concatenate([a, a], 1), jnp.concatenate([b, b], 1), info]
    )
    gains = index_weight.astype(F32).reshape(2, HALF, iheads)
    gains = jnp.moveaxis(gains, 2, 1).reshape(2, iheads * HALF)

    rows_w = nh * share
    wide = heads * HALF
    bf = jnp.bfloat16
    vmem = pl.BlockSpec(memory_space=pltpu.VMEM)
    lanes = 14 + 16 + 32
    out = pl.pallas_call(
        functools.partial(fused, ny, nh, reach, share, heads, iheads),
        out_shape=jax.ShapeDtypeStruct((1, rows), F32),
        in_specs=[pl.BlockSpec(memory_space=pltpu.SMEM)] + [vmem] * 6,
        out_specs=vmem,
        scratch_shapes=[
            pltpu.VMEM((blocks, HALF, kdim), bf),
            pltpu.VMEM((blocks, HALF, 128), bf),
            pltpu.VMEM((2, wide, kdim), bf),
            pltpu.VMEM((2, iheads * HALF, 128), bf),
            pltpu.VMEM((2, rows_w, kdim), bf),
            pltpu.VMEM((2, rows_w, 128), bf),
            pltpu.VMEM((2, rows_w, wide), F32),
            pltpu.VMEM((rows_w, 128), F32),
            pltpu.VMEM((rows_w, 128), F32),
            pltpu.VMEM((nh, share, 128), F32),
            pltpu.VMEM((nh, share, 128), F32),
            pltpu.VMEM((8, 128), F32),
            pltpu.VMEM((nh, 8, 128), F32),
            pltpu.SemaphoreType.DMA((2, lanes)),
            pltpu.SemaphoreType.DMA((2, blocks)),
            pltpu.SemaphoreType.DMA((3, nh)),
            pltpu.SemaphoreType.DMA((3, nh)),
        ],
        compiler_params=pltpu.CompilerParams(
            collective_id=0, has_side_effects=True, vmem_limit_bytes=56 * 2**20
        ),
    )(slots, latent_keys, index_keys, main_query, index_query, gains, info)
    return out.reshape(rows)


def solution(mesh):
    in_specs = (
        P("ctx", None),
        P("ctx", None),
        P("ctx", "head"),
        P("ctx", "head"),
        P("ctx", "head"),
        P(),
        P(),
    )
    return jax.shard_map(
        per_device, mesh=mesh, in_specs=in_specs, out_specs=P("ctx"), check_vma=False
    )
```

time: 287 us -> 89.4 us (0.31)
  the two profiles are of different devices: /device:TPU:24 before, /device:TPU:1 now
where the time goes in v1:
time: 89.4 us; the launch traced here: 89.1 us
  Pallas kernels  78.6 us (88%)
  local copies, waits for them, and re-layouts  6.51 us (7%)
  other arithmetic  4.01 us (4%)
    pallas_call x1, Pallas kernels, per_device(): pl.pallas_call(functools.partial(fused, ny, nh, reach, share, heads, ihea...  78.6 us
    unnamed x2, local copies, waits for them, and re-layouts  2.87 us

profile of v1, /device:TPU:1, one launch (start us, length us, event | category | flops | bytes accessed | tf_op | source)
XLA Modules:
  0.0 89.1 jit_solution(3633706355135709368)
XLA Ops:
  0.0 0.7 broadcast_multiply_fusion
  0.7 0.1 broadcast_in_dim.32
  0.8 0.1 mul.25
  0.9 0.1 iota_add_fusion
  1.0 0.1 add.105
  1.0 0.1 add.102
  1.1 0.1 add.99
  1.2 0.1 add_maximum_fusion
  1.3 0.1 max.15
  1.4 1.4 %select_reduce_fusion.slots_ref = s32[34]{0:T(128)} fusion(s32[64]{0:T(128)} %param.13, s32[34]{0:T(128)S(1)} %max.15), kind=kLoop, calls=%fused_computation.2 | loop fusion | flops 6494 | bytes 528 | tf_op jit(solution)/shard_map/reduce_sum | solution.py:321
  2.7 1.6 %gather_fusion = s32[128]{0:T(128)S(1)} fusion(s32[4096]{0:T(1024)} %param.12, s32[1024]{0:T(1024)S(1)} %pad_clamp_fusion), kind=kCustom, calls=%fused_computation | custom fusion | bytes 1536 | tf_op jit(solution)/shard_map/jit(_take)/gather | solution.py:325
  4.4 1.1 %convert_reduce_fusion = s32[128]{0:T(128)S(1)} fusion(s32[4096]{0:T(1024)} %param.12, s32[128]{0:T(128)S(1)} %and_select_fusion), kind=kLoop, calls=%fused_computation.1 | loop fusion | flops 1572736 | bytes 17408 | tf_op jit(solution)/shard_map/reduce_sum | solution.py:326
  5.5 0.8 reshape.129
  6.2 0.7 reshape.126.gain_ref
  6.9 0.1 pad_slice_fusion.1
  7.0 0.1 add_bitcast_fusion
  7.1 0.6 pad_add_fusion.info_ref
  7.7 1.7 %copy.13.lat_in = bf16[128,576]{1,0:T(8,128)(2,1)} copy(bf16[128,576]{0,1:T(8,128)(2,1)} %param.7) | data formatting | bytes 294912 | tf_op args[0]
  9.4 78.6 %shard_map.73 = f32[1,128]{1,0:T(1,128)} custom-call(s32[34]{0:T(128)} %select_reduce_fusion.slots_ref, bf16[128,576]{1,0:T(8,128)(2,1)} %copy.13.lat_in, bf16[128,128]{1,0:T(8,128)(2,1)} %idx_in.1, bf16[128,4608]{1,0:T(8,128)(2,1)} %mq_ref.1, bf16[128,512]{1,0:T(8,128)(2,1)} %iq_ref.1, f32[2,256]{1,0:T(2,128)} %reshape.126.gain_ref, ...), custom_call_target="tpu_custom_call" | custom-call | tf_op jit(solution)/shard_map/pallas_call | solution.py:342
  87.9 1.2 %copy.17 = f32[128]{0:T(128)} copy(f32[128]{0:T(128)} %bitcast.17) | data formatting | bytes 1024
  (6 shorter events, 0.0 us)

commit v2 on v1

v2 whole, which is shorter than its diff:
```python
import functools
import math

import jax
import jax.numpy as jnp
from jax import lax
from jax.experimental import pallas as pl
from jax.experimental.pallas import tpu as pltpu
from jax.sharding import PartitionSpec as P

HEADS = 128
HALF = 64
LAT = 512
ROPE = 64
FILL = -1e30
EXP_SCALE = 192.0 ** (-0.5) * math.log2(math.e)
MESH = pl.DeviceIdType.MESH
NT = (((1,), (1,)), ((), ()))
F32 = jnp.float32
BF16 = jnp.bfloat16
GROUP = 4
PAD_J = 24
FOLD = 640


def dot_nt(a, b):
    return lax.dot_general(a, b, NT, preferred_element_type=F32)


def total_of(x):
    return jnp.sum(jnp.sum(x, axis=1, keepdims=True), axis=0, keepdims=True)


def fused(
    ny, nh, reach, heads, iheads,
    lat_in, idx_in, mq_hbm, iq_in, gain_in, seg_in, order_in,
    out_ref,
    lat, idx, mraw, mq, score, bias, iq_send, iq_recv, ilhs, iwide, ipack,
    slot_v, slot_s, tsend, trecv, town, fsend, frecv,
    snd, rcv, lrcv, xsend, xrecv, local, token,
):
    kdim = LAT + ROPE
    me_c, me_h = lax.axis_index("ctx"), lax.axis_index("head")
    core = me_c % 2
    y = (me_c // 2) % ny
    xl = me_c // (2 * ny)
    xh = me_h % 2
    z = me_h // 2
    nz = nh // 2
    far = ny // 2
    half_h = nh // 2
    width = -(-reach * HALF // 128) * 128

    def ctx_of(xl_, y_, core_):
        return (xl_ * ny + y_) * 2 + core_

    up = (ctx_of(xl, (y + 1) % ny, core), me_h)
    down = (ctx_of(xl, (y + ny - 1) % ny, core), me_h)
    cross = (
        (ctx_of(1 - xl, y, core), me_h),
        (ctx_of(1 - xl, y, core), z * 2 + 1 - xh),
    )
    sibling = (ctx_of(xl, y, 1 - core), me_h)
    zup = (me_c, ((z + 1) % nz) * 2 + xh)
    zdown = (me_c, ((z + nz - 1) % nz) * 2 + xh)
    twin = (me_c, z * 2 + 1 - xh)
    near = (up, down, cross[0], cross[1], sibling, zup, zdown, twin)

    mq_copy = pltpu.make_async_copy(mq_hbm, mraw, local.at[0])
    mq_copy.start()
    barrier = pltpu.get_barrier_semaphore()
    for dev in near:
        pl.semaphore_signal(barrier, inc=1, device_id=dev, device_id_type=MESH)

    own = ctx_of(xl, y, core)
    keys = jnp.transpose(lat_in[...])
    lat[own, :, 0:LAT] = keys[0:HALF, 0:LAT]
    lat[own, :, LAT:2 * LAT] = keys[HALF:, 0:LAT]
    lat[own, :, 2 * LAT:] = jnp.concatenate([keys[0:HALF, LAT:], keys[HALF:, LAT:]], axis=1)
    for h in (0, 1):
        idx[own * 2 + h] = idx_in[h * HALF:(h + 1) * HALF, :]

    pl.semaphore_wait(barrier, len(near))

    started = []
    lanes = [0]

    def piece(b, c, h):
        if b == 0:
            return idx.at[c * 2 + h], rcv.at[c * 2 + h]
        return lat.at[c, pl.ds(h * (HALF // 2), HALF // 2)], lrcv.at[c * 2 + h]

    def send(b, c, h, dev):
        ref, sem = piece(b, c, h)
        copy = pltpu.make_async_remote_copy(
            src_ref=ref, dst_ref=ref, send_sem=snd.at[lanes[0]], recv_sem=sem,
            device_id=dev, device_id_type=MESH,
        )
        lanes[0] += 1
        copy.start()
        started.append(copy)

    def arrived(b, c, h):
        ref, sem = piece(b, c, h)
        pltpu.make_async_remote_copy(
            src_ref=ref, dst_ref=ref, send_sem=snd.at[0], recv_sem=sem,
            device_id=sibling, device_id_type=MESH,
        ).wait_recv()

    def goes(dist, h, way):
        return dist < far or (dist == far and h == way)

    def visits(s):
        for h in (0, 1):
            for way in (0, 1):
                if s == 0 and way == 1:
                    continue
                if s > 0 and not goes(s, h, way):
                    continue
                yield h, way, (y + ny - s) % ny if way == 0 else (y + s) % ny

    def ring_step(b, s):
        for h, way, yy in visits(s):
            c = ctx_of(xl, yy, core)
            if s > 0:
                arrived(b, c, h)
            for w in ((0, 1) if s == 0 else (way,)):
                if goes(s + 1, h, w):
                    send(b, c, h, up if w == 0 else down)
            send(b, c, h, cross[h])
            send(b, c, h, sibling)

    def cross_step(b, s):
        for h, way, yy in visits(s):
            c = ctx_of(1 - xl, yy, core)
            arrived(b, c, h)
            send(b, c, h, sibling)

    def sibling_wait(b):
        for xx in (0, 1):
            for yy in range(ny):
                for h in (0, 1):
                    arrived(b, ctx_of(xx, yy, 1 - core), h)

    def token_signal():
        pl.semaphore_signal(token.at[0], inc=1, device_id=zup, device_id_type=MESH)
        pl.semaphore_signal(token.at[1], inc=1, device_id=zdown, device_id_type=MESH)

    def token_wait():
        pl.semaphore_wait(token.at[0], 1)
        pl.semaphore_wait(token.at[1], 1)

    def exchange(kind, src, dst, i, start):
        to = (me_h + i) % nh
        frm = (me_h + nh - i) % nh
        copy = pltpu.make_async_remote_copy(
            src_ref=src(to), dst_ref=dst.at[me_h] if start else dst.at[frm],
            send_sem=xsend.at[kind, to],
            recv_sem=xrecv.at[kind, me_h] if start else xrecv.at[kind, frm],
            device_id=(me_c, to), device_id_type=MESH,
        )
        if start:
            copy.start()
        else:
            copy.wait()
        return 0

    def prepare_small():
        gains = jnp.concatenate(
            [gain_in[...].astype(F32), jnp.zeros((128 - iheads, 128), F32)], axis=0
        )
        gains = jnp.transpose(gains).astype(BF16)
        for i in range(8):
            rows = slice(16 * i, 16 * i + 16)
            iq_send[i, :, 0:iheads * 128] = iq_in[rows, :]
            iq_send[i, :, iheads * 128:] = gains[rows, :]
        order = order_in[...]
        blocks = order.shape[1]
        lane = lax.broadcasted_iota(jnp.int32, (1, blocks), 1)
        segs = seg_in[...].astype(F32)
        seg_row = lax.broadcasted_iota(jnp.int32, segs.shape, 0).astype(F32)
        counts = [total_of(jnp.where(segs == float(v), 1.0, 0.0)) for v in range(7)]
        for qb in (0, 1):
            mine_i = jnp.sum(jnp.where(lane == 2 * me_c + qb, order, 0), axis=1, keepdims=True)
            j = lax.broadcasted_iota(jnp.int32, (PAD_J, blocks), 0)
            want = jnp.maximum(mine_i - (reach - 1) + j, 0)
            at = lax.broadcasted_iota(jnp.int32, (PAD_J, blocks), 1)
            slot = jnp.sum(jnp.where(order == want, at, 0), axis=1, keepdims=True)
            slot = jnp.minimum(slot, blocks - 1)
            slot = jnp.broadcast_to(slot, (PAD_J, 128))
            slot_v[0, qb * PAD_J:(qb + 1) * PAD_J, :] = slot
            slot_v[1, qb * PAD_J:(qb + 1) * PAD_J, :] = slot >> 1
            slot_v[2, qb * PAD_J:(qb + 1) * PAD_J, :] = slot & 1
            mine = mine_i.astype(F32)
            first = mine - float(reach - 1)
            pair = jnp.floor(mine * 0.5)
            row = jnp.sum(jnp.where(seg_row == pair, segs, 0.0), axis=0, keepdims=True)
            row = jnp.where(mine - 2.0 * pair > 0.5, pltpu.roll(row, HALF, 1), row)
            sub = lax.broadcasted_iota(jnp.int32, (HALF, 128), 0)
            lan = lax.broadcasted_iota(jnp.int32, (HALF, 128), 1)
            seg_q = jnp.sum(jnp.where(sub == lan, row, 0.0), axis=1, keepdims=True)
            start = jnp.zeros((HALF, 1), F32)
            for v in range(7):
                start = start + jnp.where(seg_q > float(v), counts[v], 0.0)
            pos = mine * float(HALF) + lax.broadcasted_iota(
                jnp.int32, (HALF, 1), 0
            ).astype(F32)
            kp = first * float(HALF) + lax.broadcasted_iota(
                jnp.int32, (HALF, width), 1
            ).astype(F32)
            bias[qb] = jnp.where((kp >= start) & (kp <= pos), 0.0, FILL)
        copy = pltpu.make_async_copy(slot_v, slot_s, local.at[1])
        copy.start()
        copy.wait()

    def prepare_queries():
        mq_copy.wait()
        for qb in (0, 1):
            for slab in range(4):
                rows = slice(qb * HALF + slab * 16, qb * HALF + slab * 16 + 16)
                for h in range(heads):
                    x = mraw[rows, h * kdim:(h + 1) * kdim]
                    at = slab * 16 * heads + h * 16
                    mq[qb, at:at + 16, 0:LAT] = x[:, 0:LAT]
                    mq[qb, at:at + 16, LAT:] = jnp.concatenate([x[:, LAT:], x[:, LAT:]], axis=1)

    def index_queries():
        def body(i, _):
            exchange(0, lambda to: iq_send.at[to // 2], iq_recv, i, False)
            return 0
        lax.fori_loop(1, nh, body, 0)
        iq_recv[me_h] = iq_send[me_h // 2]
        odd = me_h % 2

        def pick(s, _):
            x = iq_recv[s].astype(F32)
            x = jnp.where(odd == 0, x[0:8], x[8:16])
            at = pl.multiple_of(s * iheads * 8, 16)
            ilhs[pl.ds(at, iheads * 8), :] = jnp.concatenate(
                [x[:, k * 128:(k + 1) * 128] for k in range(iheads)], axis=0
            ).astype(BF16)
            g = x[:, iheads * 128:]
            iwide[pl.ds(at, iheads * 8), :] = jnp.concatenate(
                [jnp.broadcast_to(g[:, k:k + 1], (8, 128)) for k in range(iheads)], axis=0
            )
            return 0

        lax.fori_loop(0, nh, pick, 0)

    mine_qb = me_h // half_h
    mine_row = (me_h % half_h) * 8

    def index_scores():
        rows = ilhs.shape[0]

        def scores(first, count, at):
            ks = [idx[slot_s[0, mine_qb * PAD_J + first + k, 0]] for k in range(count)]
            ks += ks[-1:] * (-count % 2)
            dots = dot_nt(ilhs[...], jnp.concatenate(ks, axis=0))
            for k in range(dots.shape[1] // 128):
                part = jnp.maximum(dots[:, k * 128:(k + 1) * 128], 0.0) * iwide[...]
                part = jnp.sum(part.reshape(rows // 8, 8, 128), axis=0)
                lo = at + k * 128
                if lo < FOLD:
                    ipack[0:8, lo:lo + 128] = part
                else:
                    ipack[8:16, lo - FOLD:lo - FOLD + 128] = part

        for first in range(0, reach, GROUP):
            scores(first, min(GROUP, reach - first), first * HALF)
        ipack[8:16, width - FOLD:] = jnp.zeros((8, 2 * FOLD - width), F32)

    def packed_bias():
        b = bias[mine_qb, pl.ds(pl.multiple_of(mine_row, 8), 8), :]
        rest = jnp.full((8, 2 * FOLD - width), FILL, F32)
        return jnp.concatenate(
            [b[:, 0:FOLD], jnp.concatenate([b[:, FOLD:], rest], axis=1)], axis=0
        )

    def both(x, op):
        return op(x[0:8], x[8:16])

    def key_block(qb, j):
        rows = lat[slot_s[1, qb * PAD_J + j, 0]]
        odd = slot_s[2, qb * PAD_J + j, 0]
        lane = lax.broadcasted_iota(jnp.int32, (HALF, 128), 1)
        second = lane * 0 + odd > 0
        second = jnp.concatenate([second] * (LAT // 128), axis=1)
        main = jnp.where(second, rows[:, LAT:2 * LAT], rows[:, 0:LAT])
        tail = rows[:, 2 * LAT:]
        tail = jnp.where(lane // HALF == odd, tail, jnp.zeros_like(tail))
        return jnp.concatenate([main, tail], axis=1)

    def scores_of(qb):
        def body(g, _):
            ks = jnp.concatenate([key_block(qb, g * GROUP + k) for k in range(GROUP)], axis=0)
            at = pl.ds(pl.multiple_of(g * GROUP * HALF, 256), GROUP * HALF)
            score[:, at] = dot_nt(mq[qb], ks)
            return 0

        lax.fori_loop(0, reach // GROUP, body, 0)
        left = reach % GROUP
        ks = [key_block(qb, reach - left + k) for k in range(left)]
        ks += ks[-1:] * (-left % 2)
        score[:, (reach - left) * HALF:] = dot_nt(mq[qb], jnp.concatenate(ks, axis=0))

    def shares_of(qb):
        def body(i, _):
            g = (me_h + i) % half_h
            d = qb * half_h + g
            b = bias[qb, pl.ds(pl.multiple_of(g * 8, 8), 8), :]
            base = (g // 2) * (16 * heads) + (g % 2) * 8
            acc = jnp.zeros((8, width), F32)
            for h in range(heads):
                s = score[pl.ds(pl.multiple_of(base + h * 16, 8), 8), :] + b
                top = jnp.max(s, axis=1, keepdims=True)
                p = jnp.exp2((s - top) * EXP_SCALE)
                acc = acc + p * (1.0 / jnp.sum(p, axis=1, keepdims=True))
            rest = jnp.zeros((8, 2 * FOLD - width), F32)
            packed = jnp.concatenate(
                [acc[:, 0:FOLD], jnp.concatenate([acc[:, FOLD:], rest], axis=1)], axis=0
            )
            tsend[d] = packed.astype(BF16)

            @pl.when(d == me_h)
            def _():
                town[...] = packed

            @pl.when(d != me_h)
            def _():
                pltpu.make_async_remote_copy(
                    src_ref=tsend.at[d], dst_ref=trecv.at[me_h],
                    send_sem=xsend.at[1, d], recv_sem=xrecv.at[1, me_h],
                    device_id=(me_c, d), device_id_type=MESH,
                ).start()

            return 0

        lax.fori_loop(1, half_h + 1, body, 0)

    ring_step(0, 0)
    ring_step(1, 0)
    token_signal()
    prepare_small()
    rounds = nz // 2
    token_wait()
    done = 1
    if done < rounds:
        token_signal()
    prepare_queries()
    for s in range(1, far + 1):
        ring_step(0, s)
        ring_step(1, s)
        for b in (0, 1):
            if done < rounds:
                token_wait()
                done += 1
                if done < rounds:
                    token_signal()
            elif done == rounds:
                lax.fori_loop(
                    1, nh,
                    lambda i, _: exchange(0, lambda to: iq_send.at[to // 2], iq_recv, i, True), 0,
                )
                done += 1
            cross_step(b, s - 1)
    index_queries()
    cross_step(0, far)
    cross_step(1, far)
    sibling_wait(0)
    index_scores()
    seen_bias = packed_bias()
    index_score = ipack[...]
    masked = index_score + seen_bias
    top = both(jnp.max(masked, axis=1, keepdims=True), jnp.maximum)
    tops = jnp.concatenate([top, top], axis=0)
    exp_sum = both(jnp.sum(jnp.exp(masked - tops), axis=1, keepdims=True), jnp.add)
    lse = top + jnp.log(exp_sum)
    sibling_wait(1)

    for qb in (0, 1):
        scores_of(qb)
        shares_of(qb)

    def add_share(i, acc):
        exchange(1, lambda to: tsend.at[to], trecv, i, False)
        return acc + trecv[(me_h + nh - i) % nh].astype(F32)

    target = lax.fori_loop(1, nh, add_share, town[...]) * (1.0 / HEADS)
    positive = target > 0.0
    logs = jnp.log(jnp.where(positive, target, 1.0))
    gain = both(
        jnp.sum(target * (logs - index_score), axis=1, keepdims=True), jnp.add
    )
    mass = both(jnp.sum(target, axis=1, keepdims=True), jnp.add)
    kl = gain + lse * mass + (1.0 - mass)
    sub = lax.broadcasted_iota(jnp.int32, (8, 128), 0)
    lan = lax.broadcasted_iota(jnp.int32, (8, 128), 1)
    mine = jnp.where(lan == 8 * me_h + sub, kl, 0.0)
    fsend[...] = mine
    lax.fori_loop(1, nh, lambda i, _: exchange(2, lambda to: fsend, frecv, i, True), 0)
    frecv[me_h] = mine
    for copy in started:
        copy.wait_send()
    lax.fori_loop(1, nh, lambda i, _: exchange(2, lambda to: fsend, frecv, i, False), 0)
    out_ref[...] = jnp.sum(jnp.sum(frecv[...], axis=0), axis=0, keepdims=True)


def per_device(
    latent_keys, index_keys, main_query, index_query, index_weight, segment_ids, block_order
):
    rows, kdim = latent_keys.shape
    nc, nh = lax.axis_size("ctx"), lax.axis_size("head")
    ny = nc // 4
    blocks = 2 * nc
    reach = nc // 2 + 1
    heads = main_query.shape[1] // kdim
    iheads = index_weight.shape[1]
    width = -(-reach * HALF // 128) * 128
    wide = heads * HALF
    vmem = pl.BlockSpec(memory_space=pltpu.VMEM)
    hbm = pl.BlockSpec(memory_space=pl.ANY)
    dma = pltpu.SemaphoreType.DMA
    out = pl.pallas_call(
        functools.partial(fused, ny, nh, reach, heads, iheads),
        out_shape=jax.ShapeDtypeStruct((1, rows), F32),
        in_specs=[vmem, vmem, hbm, vmem, vmem, vmem, vmem],
        out_specs=vmem,
        scratch_shapes=[
            pltpu.VMEM((nc, HALF, 2 * kdim), BF16),
            pltpu.VMEM((blocks, HALF, 128), BF16),
            pltpu.VMEM((rows, heads * kdim), BF16),
            pltpu.VMEM((2, wide, LAT + 2 * ROPE), BF16),
            pltpu.VMEM((wide, width), F32),
            pltpu.VMEM((2, HALF, width), F32),
            pltpu.VMEM((8, 16, iheads * 128 + 128), BF16),
            pltpu.VMEM((nh, 16, iheads * 128 + 128), BF16),
            pltpu.VMEM((nh * iheads * 8, 128), BF16),
            pltpu.VMEM((nh * iheads * 8, 128), F32),
            pltpu.VMEM((16, FOLD), F32),
            pltpu.VMEM((3, 2 * PAD_J, 128), jnp.int32),
            pltpu.SMEM((3, 2 * PAD_J, 128), jnp.int32),
            pltpu.VMEM((nh, 16, FOLD), BF16),
            pltpu.VMEM((nh, 16, FOLD), BF16),
            pltpu.VMEM((16, FOLD), F32),
            pltpu.VMEM((8, 128), F32),
            pltpu.VMEM((nh, 8, 128), F32),
            dma((4 * (7 * ny + 4),)),
            dma((blocks,)),
            dma((blocks,)),
            dma((3, nh)),
            dma((3, nh)),
            dma((2,)),
            pltpu.SemaphoreType.REGULAR((2,)),
        ],
        compiler_params=pltpu.CompilerParams(
            collective_id=0, has_side_effects=True, vmem_limit_bytes=48 * 2**20
        ),
    )(
        latent_keys.T, index_keys, main_query, index_query, index_weight.T,
        segment_ids.reshape(-1, 128), block_order.reshape(1, blocks),
    )
    return out.reshape(rows)


def solution(mesh):
    in_specs = (
        P("ctx", None),
        P("ctx", None),
        P("ctx", "head"),
        P("ctx", "head"),
        P("ctx", "head"),
        P(),
        P(),
    )
    return jax.shard_map(
        per_device, mesh=mesh, in_specs=in_specs, out_specs=P("ctx"), check_vma=False
    )
```

time: 89.4 us -> 71.4 us (0.80)
  Pallas kernels: 78.6 us -> 64.6 us
  other arithmetic: 4.01 us -> 0 us
    pallas_call x1, Pallas kernels: 78.6 us -> 64.6 us  [per_device(): pl.pallas_call(functools.partial(fused, ny, nh, reach, heads, iheads), ou...]
    unnamed x2 -> x15, local copies, waits for them, and re-layouts: 2.87 us -> 6.4 us
    reduce_sum x2 -> x0, other arithmetic: 2.43 us -> none  [the longest x1 1.35 us: per_device(): jnp.sum(jnp.where(block_order[None, :] == wanted[:, None], ids[None, :],...]
    gather x1 -> x0, local copies, waits for them, and re-layouts: 1.64 us -> none  [per_device(): seg = jnp.take(segment_ids, pos)]
    reshape x3 -> x0, local copies, waits for them, and re-layouts: 1.43 us -> none  [per_device(): gains = jnp.moveaxis(gains, 2, 1).reshape(2, iheads * HALF)]
where the time goes in v2:
time: 71.4 us; the launch traced here: 71.1 us
  Pallas kernels  64.6 us (90%)
  local copies, waits for them, and re-layouts  6.4 us (9%)
    pallas_call x1, Pallas kernels, per_device(): pl.pallas_call(functools.partial(fused, ny, nh, reach, heads, iheads), ou...  64.6 us
    unnamed x15, local copies, waits for them, and re-layouts  6.4 us

profile of v2, /device:TPU:1, one launch (start us, length us, event | category | flops | bytes accessed | tf_op | source)
XLA Modules:
  0.0 71.1 jit_solution(7835579870320244670)
XLA Ops:
  0.0 0.0 copy-start
  0.0 1.3 %copy-done = bf16[128,4608]{1,0:T(8,128)(2,1)S(1)} copy-done((bf16[128,4608]{1,0:T(8,128)(2,1)S(1)}, bf16[128,4608]{1,0:T(8,128)(2,1)}, u32[]{:S(2)}) %copy-start) | copy-done | bytes 1179672
  1.3 0.0 copy-start.1
  1.3 0.9 %copy-done.1 = bf16[128,576]{0,1:T(8,128)(2,1)S(1)} copy-done((bf16[128,576]{0,1:T(8,128)(2,1)S(1)}, bf16[128,576]{0,1:T(8,128)(2,1)}, u32[]{:S(2)}) %copy-start.1) | copy-done | bytes 147480
  2.2 0.0 copy-start.2
  2.2 0.9 %copy-done.2 = bf16[128,512]{1,0:T(8,128)(2,1)S(1)} copy-done((bf16[128,512]{1,0:T(8,128)(2,1)S(1)}, bf16[128,512]{1,0:T(8,128)(2,1)}, u32[]{:S(2)}) %copy-start.2) | copy-done | bytes 131096
  3.1 0.0 copy-start.3
  3.1 0.8 %copy-done.3 = bf16[128,128]{1,0:T(8,128)(2,1)S(1)} copy-done((bf16[128,128]{1,0:T(8,128)(2,1)S(1)}, bf16[128,128]{1,0:T(8,128)(2,1)}, u32[]{:S(2)}) %copy-start.3) | copy-done | bytes 32792
  3.8 0.0 copy-start.4
  3.8 0.7 %copy-done.4 = s32[4096]{0:T(1024)S(1)} copy-done((s32[4096]{0:T(1024)S(1)}, s32[4096]{0:T(1024)}, u32[]{:S(2)}) %copy-start.4) | copy-done | bytes 16408
  4.6 0.0 copy-start.5
  4.6 0.7 copy-done.5
  5.2 0.0 copy-start.6
  5.2 0.7 copy-done.6
  5.9 64.6 %shard_map.73 = f32[1,128]{1,0:T(1,128)S(1)} custom-call(bf16[576,128]{1,0:T(8,128)(2,1)S(1)} %bitcast.5, bf16[128,128]{1,0:T(8,128)(2,1)S(1)} %copy-done.3, bf16[128,4608]{1,0:T(8,128)(2,1)S(1)} %copy-done, bf16[128,512]{1,0:T(8,128)(2,1)S(1)} %copy-done.2, bf16[4,128]{1,0:T(4,128)(2,1)S(1)} %bitcast.7, s32[32,128]{1,0:T(8,128)S(1)} %bitcast.6, ...), custom_call_target="tpu_custom_call" | custom-call | tf_op jit(solution)/shard_map/pallas_call | solution.py:424
  70.5 0.5 copy.9
Async XLA Ops:
  0.0 1.3 %copy-start = (bf16[128,4608]{1,0:T(8,128)(2,1)S(1)}, bf16[128,4608]{1,0:T(8,128)(2,1)}, u32[]{:S(2)}) copy-start(bf16[128,4608]{1,0:T(8,128)(2,1)} %mq_hbm.1) | copy-start | bytes 3538948
  1.3 0.9 %copy-start.1 = (bf16[128,576]{0,1:T(8,128)(2,1)S(1)}, bf16[128,576]{0,1:T(8,128)(2,1)}, u32[]{:S(2)}) copy-start(bf16[128,576]{0,1:T(8,128)(2,1)} %param.7) | copy-start | bytes 442372
  2.2 0.9 %copy-start.2 = (bf16[128,512]{1,0:T(8,128)(2,1)S(1)}, bf16[128,512]{1,0:T(8,128)(2,1)}, u32[]{:S(2)}) copy-start(bf16[128,512]{1,0:T(8,128)(2,1)} %iq_in.1) | copy-start | bytes 393220
  3.1 0.8 %copy-start.3 = (bf16[128,128]{1,0:T(8,128)(2,1)S(1)}, bf16[128,128]{1,0:T(8,128)(2,1)}, u32[]{:S(2)}) copy-start(bf16[128,128]{1,0:T(8,128)(2,1)} %idx_in.1) | copy-start | bytes 98308
  3.8 0.7 %copy-start.4 = (s32[4096]{0:T(1024)S(1)}, s32[4096]{0:T(1024)}, u32[]{:S(2)}) copy-start(s32[4096]{0:T(1024)} %param.12) | copy-start | bytes 49156
  4.6 0.7 copy-start.5
  5.2 0.7 copy-start.6

commit v3 on v2

--- a/solution.py
+++ b/solution.py
@@ -20,7 +20,6 @@
 BF16 = jnp.bfloat16
 GROUP = 4
 PAD_J = 24
-FOLD = 640
 
 
 def dot_nt(a, b):
@@ -33,8 +32,9 @@
 
 def fused(
     ny, nh, reach, heads, iheads,
-    lat_in, idx_in, mq_hbm, iq_in, gain_in, seg_in, order_in,
+    lat_hbm, idx_hbm, mq_hbm, iq_hbm, gain_hbm, seg_hbm, order_hbm,
     out_ref,
+    lat_in, idx_in, iq_in, gain_in, seg_in, order_in,
     lat, idx, mraw, mq, score, bias, iq_send, iq_recv, ilhs, iwide, ipack,
     slot_v, slot_s, tsend, trecv, town, fsend, frecv,
     snd, rcv, lrcv, xsend, xrecv, local, token,
@@ -49,7 +49,8 @@
     nz = nh // 2
     far = ny // 2
     half_h = nh // 2
-    width = -(-reach * HALF // 128) * 128
+    width = (reach - 1) * HALF
+    fold = width // 2
 
     def ctx_of(xl_, y_, core_):
         return (xl_ * ny + y_) * 2 + core_
@@ -66,13 +67,24 @@
     twin = (me_c, z * 2 + 1 - xh)
     near = (up, down, cross[0], cross[1], sibling, zup, zdown, twin)
 
-    mq_copy = pltpu.make_async_copy(mq_hbm, mraw, local.at[0])
-    mq_copy.start()
+    loads = [
+        pltpu.make_async_copy(src, dst, local.at[i])
+        for i, (src, dst) in enumerate(
+            [
+                (lat_hbm, lat_in), (idx_hbm, idx_in), (iq_hbm, iq_in), (gain_hbm, gain_in),
+                (seg_hbm, seg_in), (order_hbm, order_in), (mq_hbm, mraw),
+            ]
+        )
+    ]
+    for load in loads:
+        load.start()
     barrier = pltpu.get_barrier_semaphore()
     for dev in near:
         pl.semaphore_signal(barrier, inc=1, device_id=dev, device_id_type=MESH)
 
     own = ctx_of(xl, y, core)
+    loads[0].wait()
+    loads[1].wait()
     keys = jnp.transpose(lat_in[...])
     lat[own, :, 0:LAT] = keys[0:HALF, 0:LAT]
     lat[own, :, LAT:2 * LAT] = keys[HALF:, 0:LAT]
@@ -166,6 +178,8 @@
         return 0
 
     def prepare_small():
+        for load in loads[2:6]:
+            load.wait()
         gains = jnp.concatenate(
             [gain_in[...].astype(F32), jnp.zeros((128 - iheads, 128), F32)], axis=0
         )
@@ -205,16 +219,17 @@
             pos = mine * float(HALF) + lax.broadcasted_iota(
                 jnp.int32, (HALF, 1), 0
             ).astype(F32)
-            kp = first * float(HALF) + lax.broadcasted_iota(
-                jnp.int32, (HALF, width), 1
-            ).astype(F32)
+            at = lax.broadcasted_iota(jnp.int32, (HALF, width), 1)
+            row_at = lax.broadcasted_iota(jnp.int32, (HALF, width), 0)
+            at = at + jnp.where((at < HALF) & (at <= row_at), width, 0)
+            kp = first * float(HALF) + at.astype(F32)
             bias[qb] = jnp.where((kp >= start) & (kp <= pos), 0.0, FILL)
-        copy = pltpu.make_async_copy(slot_v, slot_s, local.at[1])
+        copy = pltpu.make_async_copy(slot_v, slot_s, local.at[7])
         copy.start()
         copy.wait()
 
     def prepare_queries():
-        mq_copy.wait()
+        loads[6].wait()
         for qb in (0, 1):
             for slab in range(4):
                 rows = slice(qb * HALF + slab * 16, qb * HALF + slab * 16 + 16)
@@ -261,21 +276,24 @@
                 part = jnp.maximum(dots[:, k * 128:(k + 1) * 128], 0.0) * iwide[...]
                 part = jnp.sum(part.reshape(rows // 8, 8, 128), axis=0)
                 lo = at + k * 128
-                if lo < FOLD:
+                if lo < fold:
                     ipack[0:8, lo:lo + 128] = part
                 else:
-                    ipack[8:16, lo - FOLD:lo - FOLD + 128] = part
-
-        for first in range(0, reach, GROUP):
-            scores(first, min(GROUP, reach - first), first * HALF)
-        ipack[8:16, width - FOLD:] = jnp.zeros((8, 2 * FOLD - width), F32)
+                    ipack[8:16, lo - fold:lo - fold + 128] = part
+
+        for first in range(0, reach - 1, GROUP):
+            scores(first, GROUP, first * HALF)
+        last = ipack[0:8, 0:128]
+        scores(reach - 1, 1, 0)
+        lane = lax.broadcasted_iota(jnp.int32, (8, 128), 1)
+        row = mine_row + lax.broadcasted_iota(jnp.int32, (8, 128), 0)
+        ipack[0:8, 0:128] = jnp.where((lane < HALF) & (lane <= row), ipack[0:8, 0:128], last)
+
+    def packed(x):
+        return jnp.concatenate([x[:, 0:fold], x[:, fold:]], axis=0)
 
     def packed_bias():
-        b = bias[mine_qb, pl.ds(pl.multiple_of(mine_row, 8), 8), :]
-        rest = jnp.full((8, 2 * FOLD - width), FILL, F32)
-        return jnp.concatenate(
-            [b[:, 0:FOLD], jnp.concatenate([b[:, FOLD:], rest], axis=1)], axis=0
-        )
+        return packed(bias[mine_qb, pl.ds(pl.multiple_of(mine_row, 8), 8), :])
 
     def both(x, op):
         return op(x[0:8], x[8:16])
@@ -298,11 +316,13 @@
             score[:, at] = dot_nt(mq[qb], ks)
             return 0
 
-        lax.fori_loop(0, reach // GROUP, body, 0)
-        left = reach % GROUP
-        ks = [key_block(qb, reach - left + k) for k in range(left)]
-        ks += ks[-1:] * (-left % 2)
-        score[:, (reach - left) * HALF:] = dot_nt(mq[qb], jnp.concatenate(ks, axis=0))
+        lax.fori_loop(0, (reach - 1) // GROUP, body, 0)
+        last = key_block(qb, reach - 1)
+        s = dot_nt(mq[qb], jnp.concatenate([last, last], axis=0))
+        at = lax.broadcasted_iota(jnp.int32, s.shape, 0)
+        row = at // (16 * heads) * 16 + at % 16
+        lane = lax.broadcasted_iota(jnp.int32, s.shape, 1)
+        score[:, 0:128] = jnp.where((lane < HALF) & (lane <= row), s, score[:, 0:128])
 
     def shares_of(qb):
         def body(i, _):
@@ -316,15 +336,12 @@
                 top = jnp.max(s, axis=1, keepdims=True)
                 p = jnp.exp2((s - top) * EXP_SCALE)
                 acc = acc + p * (1.0 / jnp.sum(p, axis=1, keepdims=True))
-            rest = jnp.zeros((8, 2 * FOLD - width), F32)
-            packed = jnp.concatenate(
-                [acc[:, 0:FOLD], jnp.concatenate([acc[:, FOLD:], rest], axis=1)], axis=0
-            )
-            tsend[d] = packed.astype(BF16)
+            share = packed(acc)
+            tsend[d] = share.astype(BF16)
 
             @pl.when(d == me_h)
             def _():
-                town[...] = packed
+                town[...] = share
 
             @pl.when(d != me_h)
             def _():
@@ -348,27 +365,35 @@
     if done < rounds:
         token_signal()
     prepare_queries()
-    for s in range(1, far + 1):
-        ring_step(0, s)
-        ring_step(1, s)
-        for b in (0, 1):
-            if done < rounds:
-                token_wait()
-                done += 1
-                if done < rounds:
-                    token_signal()
-            elif done == rounds:
+
+    def token_round():
+        token_wait()
+        done_rounds[0] += 1
+        if done_rounds[0] < rounds:
+            token_signal()
+
+    done_rounds = [done]
+    steps = [(0, s) for s in range(1, far + 1)]
+    for s in range(1, far):
+        steps.insert(min(3 * s - 1, len(steps)), (1, s))
+    for n, (b, s) in enumerate(steps):
+        ring_step(b, s)
+        cross_step(b, s - 1)
+        if n == len(steps) - 2:
+            cross_step(0, far)
+        if done_rounds[0] < rounds:
+            token_round()
+            if done_rounds[0] == rounds:
                 lax.fori_loop(
                     1, nh,
                     lambda i, _: exchange(0, lambda to: iq_send.at[to // 2], iq_recv, i, True), 0,
                 )
-                done += 1
-            cross_step(b, s - 1)
     index_queries()
-    cross_step(0, far)
-    cross_step(1, far)
     sibling_wait(0)
     index_scores()
+    ring_step(1, far)
+    cross_step(1, far - 1)
+    cross_step(1, far)
     seen_bias = packed_bias()
     index_score = ipack[...]
     masked = index_score + seen_bias
@@ -416,7 +441,8 @@
     reach = nc // 2 + 1
     heads = main_query.shape[1] // kdim
     iheads = index_weight.shape[1]
-    width = -(-reach * HALF // 128) * 128
+    width = (reach - 1) * HALF
+    fold = width // 2
     wide = heads * HALF
     vmem = pl.BlockSpec(memory_space=pltpu.VMEM)
     hbm = pl.BlockSpec(memory_space=pl.ANY)
@@ -424,9 +450,15 @@
     out = pl.pallas_call(
         functools.partial(fused, ny, nh, reach, heads, iheads),
         out_shape=jax.ShapeDtypeStruct((1, rows), F32),
-        in_specs=[vmem, vmem, hbm, vmem, vmem, vmem, vmem],
+        in_specs=[hbm] * 7,
         out_specs=vmem,
         scratch_shapes=[
+            pltpu.VMEM((kdim, rows), BF16),
+            pltpu.VMEM((rows, 128), BF16),
+            pltpu.VMEM((rows, iheads * 128), BF16),
+            pltpu.VMEM((iheads, rows), BF16),
+            pltpu.VMEM((blocks * HALF // 128, 128), jnp.int32),
+            pltpu.VMEM((1, blocks), jnp.int32),
             pltpu.VMEM((nc, HALF, 2 * kdim), BF16),
             pltpu.VMEM((blocks, HALF, 128), BF16),
             pltpu.VMEM((rows, heads * kdim), BF16),
@@ -437,12 +469,12 @@
             pltpu.VMEM((nh, 16, iheads * 128 + 128), BF16),
             pltpu.VMEM((nh * iheads * 8, 128), BF16),
             pltpu.VMEM((nh * iheads * 8, 128), F32),
-            pltpu.VMEM((16, FOLD), F32),
+            pltpu.VMEM((16, fold), F32),
             pltpu.VMEM((3, 2 * PAD_J, 128), jnp.int32),
             pltpu.SMEM((3, 2 * PAD_J, 128), jnp.int32),
-            pltpu.VMEM((nh, 16, FOLD), BF16),
-            pltpu.VMEM((nh, 16, FOLD), BF16),
-            pltpu.VMEM((16, FOLD), F32),
+            pltpu.VMEM((nh, 16, fold), BF16),
+            pltpu.VMEM((nh, 16, fold), BF16),
+            pltpu.VMEM((16, fold), F32),
             pltpu.VMEM((8, 128), F32),
             pltpu.VMEM((nh, 8, 128), F32),
             dma((4 * (7 * ny + 4),)),
@@ -450,11 +482,11 @@
             dma((blocks,)),
             dma((3, nh)),
             dma((3, nh)),
-            dma((2,)),
+            dma((8,)),
             pltpu.SemaphoreType.REGULAR((2,)),
         ],
         compiler_params=pltpu.CompilerParams(
-            collective_id=0, has_side_effects=True, vmem_limit_bytes=48 * 2**20
+            collective_id=0, has_side_effects=True, vmem_limit_bytes=60 * 2**20
         ),
     )(
         latent_keys.T, index_keys, main_query, index_query, index_weight.T,

time: 71.4 us -> 68.8 us (0.964)
  local copies, waits for them, and re-layouts: 6.4 us -> 1.19 us
  Pallas kernels: 64.6 us -> 67.5 us
    unnamed x15 -> x1, local copies, waits for them, and re-layouts: 6.4 us -> 1.19 us
    pallas_call x1, Pallas kernels: 64.6 us -> 67.5 us  [per_device(): pl.pallas_call(functools.partial(fused, ny, nh, reach, heads, iheads), ou...]
where the time goes in v3:
time: 68.8 us; the launch traced here: 68.7 us
  Pallas kernels  67.5 us (98%)
  local copies, waits for them, and re-layouts  1.19 us (2%)
    pallas_call x1, Pallas kernels, per_device(): pl.pallas_call(functools.partial(fused, ny, nh, reach, heads, iheads), ou...  67.5 us

profile of v3, /device:TPU:1, one launch (start us, length us, event | category | flops | bytes accessed | tf_op | source)
XLA Modules:
  0.0 68.7 jit_solution(1042173759604699928)
XLA Ops:
  0.0 67.5 %shard_map.73 = f32[1,128]{1,0:T(1,128)} custom-call(bf16[576,128]{1,0:T(8,128)(2,1)} %bitcast.5, bf16[128,128]{1,0:T(8,128)(2,1)} %idx_hbm.1, bf16[128,4608]{1,0:T(8,128)(2,1)} %mq_hbm.1, bf16[128,512]{1,0:T(8,128)(2,1)} %iq_hbm.1, bf16[4,128]{1,0:T(4,128)(2,1)} %bitcast.7, s32[32,128]{1,0:T(8,128)} %bitcast.6, s32[1,64]{1,0:T(1,128)} %bitcast.8), custom_call_target="tpu_custom_call" | custom-call | tf_op jit(solution)/shard_map/pallas_call | solution.py:450
  67.5 1.2 %copy.9 = f32[128]{0:T(128)} copy(f32[128]{0:T(128)} %bitcast.9) | data formatting | bytes 1024

commit v4 on v3

--- a/solution.py
+++ b/solution.py
@@ -35,9 +35,9 @@
     lat_hbm, idx_hbm, mq_hbm, iq_hbm, gain_hbm, seg_hbm, order_hbm,
     out_ref,
     lat_in, idx_in, iq_in, gain_in, seg_in, order_in,
-    lat, idx, mraw, mq, score, bias, iq_send, iq_recv, ilhs, iwide, ipack,
+    lat, mraw, mq, score, bias, iq_send, iq_recv, ilhs, iwide, ipack,
     slot_v, slot_s, tsend, trecv, town, fsend, frecv,
-    snd, rcv, lrcv, xsend, xrecv, local, token,
+    snd, rcv, xsend, xrecv, local, token,
 ):
     kdim = LAT + ROPE
     me_c, me_h = lax.axis_index("ctx"), lax.axis_index("head")
@@ -88,32 +88,29 @@
     keys = jnp.transpose(lat_in[...])
     lat[own, :, 0:LAT] = keys[0:HALF, 0:LAT]
     lat[own, :, LAT:2 * LAT] = keys[HALF:, 0:LAT]
-    lat[own, :, 2 * LAT:] = jnp.concatenate([keys[0:HALF, LAT:], keys[HALF:, LAT:]], axis=1)
+    lat[own, :, 2 * LAT:2 * kdim] = jnp.concatenate([keys[0:HALF, LAT:], keys[HALF:, LAT:]], axis=1)
     for h in (0, 1):
-        idx[own * 2 + h] = idx_in[h * HALF:(h + 1) * HALF, :]
+        at = 2 * kdim + h * 128
+        lat[own, :, at:at + 128] = idx_in[h * HALF:(h + 1) * HALF, :]
 
     pl.semaphore_wait(barrier, len(near))
 
     started = []
-    lanes = [0]
-
-    def piece(b, c, h):
-        if b == 0:
-            return idx.at[c * 2 + h], rcv.at[c * 2 + h]
-        return lat.at[c, pl.ds(h * (HALF // 2), HALF // 2)], lrcv.at[c * 2 + h]
-
-    def send(b, c, h, dev):
-        ref, sem = piece(b, c, h)
+
+    def piece(c, h):
+        return lat.at[c, pl.ds(h * (HALF // 2), HALF // 2)], rcv.at[c * 2 + h]
+
+    def send(c, h, dev):
+        ref, sem = piece(c, h)
         copy = pltpu.make_async_remote_copy(
-            src_ref=ref, dst_ref=ref, send_sem=snd.at[lanes[0]], recv_sem=sem,
+            src_ref=ref, dst_ref=ref, send_sem=snd.at[len(started)], recv_sem=sem,
             device_id=dev, device_id_type=MESH,
         )
-        lanes[0] += 1
         copy.start()
         started.append(copy)
 
-    def arrived(b, c, h):
-        ref, sem = piece(b, c, h)
+    def arrived(c, h):
+        ref, sem = piece(c, h)
         pltpu.make_async_remote_copy(
             src_ref=ref, dst_ref=ref, send_sem=snd.at[0], recv_sem=sem,
             device_id=sibling, device_id_type=MESH,
@@ -131,28 +128,28 @@
                     continue
                 yield h, way, (y + ny - s) % ny if way == 0 else (y + s) % ny
 
-    def ring_step(b, s):
+    def ring_step(s):
         for h, way, yy in visits(s):
             c = ctx_of(xl, yy, core)
             if s > 0:
-                arrived(b, c, h)
+                arrived(c, h)
             for w in ((0, 1) if s == 0 else (way,)):
                 if goes(s + 1, h, w):
-                    send(b, c, h, up if w == 0 else down)
-            send(b, c, h, cross[h])
-            send(b, c, h, sibling)
-
-    def cross_step(b, s):
+                    send(c, h, up if w == 0 else down)
+            send(c, h, cross[h])
+            send(c, h, sibling)
+
+    def cross_step(s):
         for h, way, yy in visits(s):
             c = ctx_of(1 - xl, yy, core)
-            arrived(b, c, h)
-            send(b, c, h, sibling)
-
-    def sibling_wait(b):
+            arrived(c, h)
+            send(c, h, sibling)
+
+    def sibling_wait():
         for xx in (0, 1):
             for yy in range(ny):
                 for h in (0, 1):
-                    arrived(b, ctx_of(xx, yy, 1 - core), h)
+                    arrived(ctx_of(xx, yy, 1 - core), h)
 
     def token_signal():
         pl.semaphore_signal(token.at[0], inc=1, device_id=zup, device_id_type=MESH)
@@ -162,7 +159,8 @@
         pl.semaphore_wait(token.at[0], 1)
         pl.semaphore_wait(token.at[1], 1)
 
-    def exchange(kind, src, dst, i, start):
+    def exchange(kind, src, dst, k, start):
+        i = half_h + (k // 2) * (2 * (k % 2) - 1)
         to = (me_h + i) % nh
         frm = (me_h + nh - i) % nh
         copy = pltpu.make_async_remote_copy(
@@ -268,8 +266,16 @@
     def index_scores():
         rows = ilhs.shape[0]
 
+        def block(j):
+            rows = lat[slot_s[1, mine_qb * PAD_J + j, 0]]
+            odd = slot_s[2, mine_qb * PAD_J + j, 0]
+            lane = lax.broadcasted_iota(jnp.int32, (HALF, 128), 1)
+            return jnp.where(
+                lane * 0 + odd > 0, rows[:, 2 * kdim + 128:], rows[:, 2 * kdim:2 * kdim + 128]
+            )
+
         def scores(first, count, at):
-            ks = [idx[slot_s[0, mine_qb * PAD_J + first + k, 0]] for k in range(count)]
+            ks = [block(first + k) for k in range(count)]
             ks += ks[-1:] * (-count % 2)
             dots = dot_nt(ilhs[...], jnp.concatenate(ks, axis=0))
             for k in range(dots.shape[1] // 128):
@@ -305,7 +311,7 @@
         second = lane * 0 + odd > 0
         second = jnp.concatenate([second] * (LAT // 128), axis=1)
         main = jnp.where(second, rows[:, LAT:2 * LAT], rows[:, 0:LAT])
-        tail = rows[:, 2 * LAT:]
+        tail = rows[:, 2 * LAT:2 * kdim]
         tail = jnp.where(lane // HALF == odd, tail, jnp.zeros_like(tail))
         return jnp.concatenate([main, tail], axis=1)
 
@@ -353,10 +359,9 @@
 
             return 0
 
-        lax.fori_loop(1, half_h + 1, body, 0)
-
-    ring_step(0, 0)
-    ring_step(1, 0)
+        lax.fori_loop(1, half_h + 1, body, 0, unroll=2)
+
+    ring_step(0)
     token_signal()
     prepare_small()
     rounds = nz // 2
@@ -365,35 +370,30 @@
     if done < rounds:
         token_signal()
     prepare_queries()
-
-    def token_round():
-        token_wait()
-        done_rounds[0] += 1
-        if done_rounds[0] < rounds:
-            token_signal()
-
-    done_rounds = [done]
-    steps = [(0, s) for s in range(1, far + 1)]
-    for s in range(1, far):
-        steps.insert(min(3 * s - 1, len(steps)), (1, s))
-    for n, (b, s) in enumerate(steps):
-        ring_step(b, s)
-        cross_step(b, s - 1)
-        if n == len(steps) - 2:
-            cross_step(0, far)
-        if done_rounds[0] < rounds:
-            token_round()
-            if done_rounds[0] == rounds:
-                lax.fori_loop(
-                    1, nh,
-                    lambda i, _: exchange(0, lambda to: iq_send.at[to // 2], iq_recv, i, True), 0,
-                )
+    for s in range(1, far + 1):
+        ring_step(s)
+        for _ in range(2):
+            if done < rounds:
+                token_wait()
+                done += 1
+                if done < rounds:
+                    token_signal()
+                else:
+                    lax.fori_loop(
+                        1, nh,
+                        lambda i, _: exchange(0, lambda to: iq_send.at[to // 2], iq_recv, i, True),
+                        0,
+                    )
+        cross_step(s - 1)
+    cross_step(far)
+    sibling_wait()
+
+    for qb in (0, 1):
+        scores_of(qb)
+        shares_of(qb)
+
     index_queries()
-    sibling_wait(0)
     index_scores()
-    ring_step(1, far)
-    cross_step(1, far - 1)
-    cross_step(1, far)
     seen_bias = packed_bias()
     index_score = ipack[...]
     masked = index_score + seen_bias
@@ -401,15 +401,12 @@
     tops = jnp.concatenate([top, top], axis=0)
     exp_sum = both(jnp.sum(jnp.exp(masked - tops), axis=1, keepdims=True), jnp.add)
     lse = top + jnp.log(exp_sum)
-    sibling_wait(1)
-
-    for qb in (0, 1):
-        scores_of(qb)
-        shares_of(qb)
+    for copy in started:
+        copy.wait_send()
 
     def add_share(i, acc):
         exchange(1, lambda to: tsend.at[to], trecv, i, False)
-        return acc + trecv[(me_h + nh - i) % nh].astype(F32)
+        return acc + trecv[(me_h + nh - (half_h + (i // 2) * (2 * (i % 2) - 1))) % nh].astype(F32)
 
     target = lax.fori_loop(1, nh, add_share, town[...]) * (1.0 / HEADS)
     positive = target > 0.0
@@ -425,8 +422,6 @@
     fsend[...] = mine
     lax.fori_loop(1, nh, lambda i, _: exchange(2, lambda to: fsend, frecv, i, True), 0)
     frecv[me_h] = mine
-    for copy in started:
-        copy.wait_send()
     lax.fori_loop(1, nh, lambda i, _: exchange(2, lambda to: fsend, frecv, i, False), 0)
     out_ref[...] = jnp.sum(jnp.sum(frecv[...], axis=0), axis=0, keepdims=True)
 
@@ -459,8 +454,7 @@
             pltpu.VMEM((iheads, rows), BF16),
             pltpu.VMEM((blocks * HALF // 128, 128), jnp.int32),
             pltpu.VMEM((1, blocks), jnp.int32),
-            pltpu.VMEM((nc, HALF, 2 * kdim), BF16),
-            pltpu.VMEM((blocks, HALF, 128), BF16),
+            pltpu.VMEM((nc, HALF, 2 * kdim + 256), BF16),
             pltpu.VMEM((rows, heads * kdim), BF16),
             pltpu.VMEM((2, wide, LAT + 2 * ROPE), BF16),
             pltpu.VMEM((wide, width), F32),
@@ -477,8 +471,7 @@
             pltpu.VMEM((16, fold), F32),
             pltpu.VMEM((8, 128), F32),
             pltpu.VMEM((nh, 8, 128), F32),
-            dma((4 * (7 * ny + 4),)),
-            dma((blocks,)),
+            dma((2 * (ny - 1) + 6 * ny,)),
             dma((blocks,)),
             dma((3, nh)),
             dma((3, nh)),

time: 68.8 us -> 61.7 us (0.90)
  Pallas kernels: 67.5 us -> 60.3 us
    pallas_call x1, Pallas kernels: 67.5 us -> 60.3 us  [per_device(): pl.pallas_call(functools.partial(fused, ny, nh, reach, heads, iheads), ou...]
where the time goes in v4:
time: 61.7 us; the launch traced here: 61.5 us
  Pallas kernels  60.3 us (98%)
  local copies, waits for them, and re-layouts  1.19 us (2%)
    pallas_call x1, Pallas kernels, per_device(): pl.pallas_call(functools.partial(fused, ny, nh, reach, heads, iheads), ou...  60.3 us

profile of v4, /device:TPU:1, one launch (start us, length us, event | category | flops | bytes accessed | tf_op | source)
XLA Modules:
  0.0 61.5 jit_solution(6809068808468336885)
XLA Ops:
  0.0 60.3 %shard_map.73 = f32[1,128]{1,0:T(1,128)} custom-call(bf16[576,128]{1,0:T(8,128)(2,1)} %bitcast.5, bf16[128,128]{1,0:T(8,128)(2,1)} %idx_hbm.1, bf16[128,4608]{1,0:T(8,128)(2,1)} %mq_hbm.1, bf16[128,512]{1,0:T(8,128)(2,1)} %iq_hbm.1, bf16[4,128]{1,0:T(4,128)(2,1)} %bitcast.7, s32[32,128]{1,0:T(8,128)} %bitcast.6, s32[1,64]{1,0:T(1,128)} %bitcast.8), custom_call_target="tpu_custom_call" | custom-call | tf_op jit(solution)/shard_map/pallas_call | solution.py:445
  60.4 1.2 %copy.9 = f32[128]{0:T(128)} copy(f32[128]{0:T(128)} %bitcast.9) | data formatting | bytes 1024

commit v5 on v4

--- a/solution.py
+++ b/solution.py
@@ -19,6 +19,7 @@
 F32 = jnp.float32
 BF16 = jnp.bfloat16
 GROUP = 4
+UNROLL_M = 4
 PAD_J = 24
 
 
@@ -36,7 +37,7 @@
     out_ref,
     lat_in, idx_in, iq_in, gain_in, seg_in, order_in,
     lat, mraw, mq, score, bias, iq_send, iq_recv, ilhs, iwide, ipack,
-    slot_v, slot_s, tsend, trecv, town, fsend, frecv,
+    slot_v, slot_s, tsend, trecv, town, kept, fsend, frecv,
     snd, rcv, xsend, xrecv, local, token,
 ):
     kdim = LAT + ROPE
@@ -322,7 +323,7 @@
             score[:, at] = dot_nt(mq[qb], ks)
             return 0
 
-        lax.fori_loop(0, (reach - 1) // GROUP, body, 0)
+        lax.fori_loop(0, (reach - 1) // GROUP, body, 0, unroll=UNROLL_M)
         last = key_block(qb, reach - 1)
         s = dot_nt(mq[qb], jnp.concatenate([last, last], axis=0))
         at = lax.broadcasted_iota(jnp.int32, s.shape, 0)
@@ -331,23 +332,29 @@
         score[:, 0:128] = jnp.where((lane < HALF) & (lane <= row), s, score[:, 0:128])
 
     def shares_of(qb):
-        def body(i, _):
-            g = (me_h + i) % half_h
-            d = qb * half_h + g
-            b = bias[qb, pl.ds(pl.multiple_of(g * 8, 8), 8), :]
-            base = (g // 2) * (16 * heads) + (g % 2) * 8
-            acc = jnp.zeros((8, width), F32)
+        def slab(i, _):
+            b = bias[qb, pl.ds(pl.multiple_of(i * 16, 16), 16), :]
+            acc = jnp.zeros((16, width), F32)
             for h in range(heads):
-                s = score[pl.ds(pl.multiple_of(base + h * 16, 8), 8), :] + b
+                at = pl.multiple_of(i * (16 * heads) + h * 16, 16)
+                s = score[pl.ds(at, 16), :] + b
                 top = jnp.max(s, axis=1, keepdims=True)
                 p = jnp.exp2((s - top) * EXP_SCALE)
                 acc = acc + p * (1.0 / jnp.sum(p, axis=1, keepdims=True))
-            share = packed(acc)
-            tsend[d] = share.astype(BF16)
-
-            @pl.when(d == me_h)
-            def _():
-                town[...] = share
+            for k in (0, 1):
+                share = packed(acc[8 * k:8 * k + 8])
+                kept[2 * i + k] = share
+                tsend[qb * half_h + 2 * i + k] = share.astype(BF16)
+            return 0
+
+        lax.fori_loop(0, 4, slab, 0, unroll=4)
+
+        @pl.when(mine_qb == qb)
+        def _():
+            town[...] = kept[me_h % half_h]
+
+        def share_send(i, _):
+            d = qb * half_h + (me_h + i) % half_h
 
             @pl.when(d != me_h)
             def _():
@@ -359,7 +366,7 @@
 
             return 0
 
-        lax.fori_loop(1, half_h + 1, body, 0, unroll=2)
+        lax.fori_loop(1, half_h + 1, share_send, 0)
 
     ring_step(0)
     token_signal()
@@ -439,6 +446,7 @@
     width = (reach - 1) * HALF
     fold = width // 2
     wide = heads * HALF
+    half_h = nh // 2
     vmem = pl.BlockSpec(memory_space=pltpu.VMEM)
     hbm = pl.BlockSpec(memory_space=pl.ANY)
     dma = pltpu.SemaphoreType.DMA
@@ -469,6 +477,7 @@
             pltpu.VMEM((nh, 16, fold), BF16),
             pltpu.VMEM((nh, 16, fold), BF16),
             pltpu.VMEM((16, fold), F32),
+            pltpu.VMEM((half_h, 16, fold), F32),
             pltpu.VMEM((8, 128), F32),
             pltpu.VMEM((nh, 8, 128), F32),
             dma((2 * (ny - 1) + 6 * ny,)),

time: 61.7 us -> 59.4 us (0.963)
  Pallas kernels: 60.3 us -> 58.1 us
    pallas_call x1, Pallas kernels: 60.3 us -> 58.1 us  [per_device(): pl.pallas_call(functools.partial(fused, ny, nh, reach, heads, iheads), ou...]
where the time goes in v5:
time: 59.4 us; the launch traced here: 59.3 us
  Pallas kernels  58.1 us (98%)
  local copies, waits for them, and re-layouts  1.19 us (2%)
    pallas_call x1, Pallas kernels, per_device(): pl.pallas_call(functools.partial(fused, ny, nh, reach, heads, iheads), ou...  58.1 us
    unnamed x1, local copies, waits for them, and re-layouts  1.19 us

profile of v5, /device:TPU:1, one launch (start us, length us, event | category | flops | bytes accessed | tf_op | source)
XLA Modules:
  0.0 59.3 jit_solution(12588411435322139712)
XLA Ops:
  0.0 58.1 %shard_map.73 = f32[1,128]{1,0:T(1,128)} custom-call(bf16[576,128]{1,0:T(8,128)(2,1)} %bitcast.5, bf16[128,128]{1,0:T(8,128)(2,1)} %idx_hbm.1, bf16[128,4608]{1,0:T(8,128)(2,1)} %mq_hbm.1, bf16[128,512]{1,0:T(8,128)(2,1)} %iq_hbm.1, bf16[4,128]{1,0:T(4,128)(2,1)} %bitcast.7, s32[32,128]{1,0:T(8,128)} %bitcast.6, s32[1,64]{1,0:T(1,128)} %bitcast.8), custom_call_target="tpu_custom_call" | custom-call | tf_op jit(solution)/shard_map/pallas_call | solution.py:453
  58.1 1.2 %copy.9 = f32[128]{0:T(128)} copy(f32[128]{0:T(128)} %bitcast.9) | data formatting | bytes 1024

commit v6 on v5

--- a/solution.py
+++ b/solution.py
@@ -160,10 +160,13 @@
         pl.semaphore_wait(token.at[0], 1)
         pl.semaphore_wait(token.at[1], 1)
 
+    def spread(k):
+        return half_h + lax.div(k, 2) * (2 * lax.rem(k, 2) - 1)
+
     def exchange(kind, src, dst, k, start):
-        i = half_h + (k // 2) * (2 * (k % 2) - 1)
-        to = (me_h + i) % nh
-        frm = (me_h + nh - i) % nh
+        i = spread(k)
+        to = lax.rem(me_h + i, nh)
+        frm = lax.rem(me_h + nh - i, nh)
         copy = pltpu.make_async_remote_copy(
             src_ref=src(to), dst_ref=dst.at[me_h] if start else dst.at[frm],
             send_sem=xsend.at[kind, to],
@@ -392,6 +395,7 @@
                         0,
                     )
         cross_step(s - 1)
+    index_queries()
     cross_step(far)
     sibling_wait()
 
@@ -399,7 +403,6 @@
         scores_of(qb)
         shares_of(qb)
 
-    index_queries()
     index_scores()
     seen_bias = packed_bias()
     index_score = ipack[...]
@@ -412,8 +415,8 @@
         copy.wait_send()
 
     def add_share(i, acc):
-        exchange(1, lambda to: tsend.at[to], trecv, i, False)
-        return acc + trecv[(me_h + nh - (half_h + (i // 2) * (2 * (i % 2) - 1))) % nh].astype(F32)
+        exchange(1, lambda to: tsend.at[to], trecv, nh - i, False)
+        return acc + trecv[lax.rem(me_h + nh - spread(nh - i), nh)].astype(F32)
 
     target = lax.fori_loop(1, nh, add_share, town[...]) * (1.0 / HEADS)
     positive = target > 0.0

time: 59.4 us -> 59.5 us (level)
  no operation moved by 1% of the time
where the time goes in v6:
time: 59.5 us; the launch traced here: 59.4 us
  Pallas kernels  58.2 us (98%)
  local copies, waits for them, and re-layouts  1.19 us (2%)
    pallas_call x1, Pallas kernels, per_device(): pl.pallas_call(functools.partial(fused, ny, nh, reach, heads, iheads), ou...  58.2 us
    unnamed x1, local copies, waits for them, and re-layouts  1.19 us

profile of v6, /device:TPU:1, one launch (start us, length us, event | category | flops | bytes accessed | tf_op | source)
XLA Modules:
  0.0 59.4 jit_solution(590197159515844634)
XLA Ops:
  0.0 58.2 %shard_map.73 = f32[1,128]{1,0:T(1,128)} custom-call(bf16[576,128]{1,0:T(8,128)(2,1)} %bitcast.5, bf16[128,128]{1,0:T(8,128)(2,1)} %idx_hbm.1, bf16[128,4608]{1,0:T(8,128)(2,1)} %mq_hbm.1, bf16[128,512]{1,0:T(8,128)(2,1)} %iq_hbm.1, bf16[4,128]{1,0:T(4,128)(2,1)} %bitcast.7, s32[32,128]{1,0:T(8,128)} %bitcast.6, s32[1,64]{1,0:T(1,128)} %bitcast.8), custom_call_target="tpu_custom_call" | custom-call | tf_op jit(solution)/shard_map/pallas_call | solution.py:456
  58.2 1.2 %copy.9 = f32[128]{0:T(128)} copy(f32[128]{0:T(128)} %bitcast.9) | data formatting | bytes 1024

commit v7 on v6

--- a/solution.py
+++ b/solution.py
@@ -334,7 +334,7 @@
         lane = lax.broadcasted_iota(jnp.int32, s.shape, 1)
         score[:, 0:128] = jnp.where((lane < HALF) & (lane <= row), s, score[:, 0:128])
 
-    def shares_of(qb):
+    def shares_of(qb, mine):
         def slab(i, _):
             b = bias[qb, pl.ds(pl.multiple_of(i * 16, 16), 16), :]
             acc = jnp.zeros((16, width), F32)
@@ -352,24 +352,24 @@
 
         lax.fori_loop(0, 4, slab, 0, unroll=4)
 
-        @pl.when(mine_qb == qb)
-        def _():
-            town[...] = kept[me_h % half_h]
-
-        def share_send(i, _):
-            d = qb * half_h + (me_h + i) % half_h
-
-            @pl.when(d != me_h)
-            def _():
-                pltpu.make_async_remote_copy(
-                    src_ref=tsend.at[d], dst_ref=trecv.at[me_h],
-                    send_sem=xsend.at[1, d], recv_sem=xrecv.at[1, me_h],
-                    device_id=(me_c, d), device_id_type=MESH,
-                ).start()
-
+        here = lax.rem(me_h, half_h)
+        if mine:
+            town[...] = kept[here]
+
+        def share_send(k, _):
+            if mine:
+                off = half_h // 2 + lax.div(k, 2) * (2 * lax.rem(k, 2) - 1)
+            else:
+                off = lax.div(k + 1, 2) * (1 - 2 * lax.rem(k, 2))
+            d = qb * half_h + lax.rem(here + half_h + off, half_h)
+            pltpu.make_async_remote_copy(
+                src_ref=tsend.at[d], dst_ref=trecv.at[me_h],
+                send_sem=xsend.at[1, d], recv_sem=xrecv.at[1, me_h],
+                device_id=(me_c, d), device_id_type=MESH,
+            ).start()
             return 0
 
-        lax.fori_loop(1, half_h + 1, share_send, 0)
+        lax.fori_loop(1 if mine else 0, half_h, share_send, 0)
 
     ring_step(0)
     token_signal()
@@ -399,9 +399,10 @@
     cross_step(far)
     sibling_wait()
 
-    for qb in (0, 1):
-        scores_of(qb)
-        shares_of(qb)
+    for mine in (False, True):
+        block = mine_qb if mine else 1 - mine_qb
+        scores_of(block)
+        shares_of(block, mine)
 
     index_scores()
     seen_bias = packed_bias()

time: 59.5 us -> 60.1 us (1.010)
  no operation moved by 1% of the time
where the time goes in v7:
time: 60.1 us; the launch traced here: 59.9 us
  Pallas kernels  58.7 us (98%)
  local copies, waits for them, and re-layouts  1.19 us (2%)
    pallas_call x1, Pallas kernels, per_device(): pl.pallas_call(functools.partial(fused, ny, nh, reach, heads, iheads), ou...  58.7 us

profile of v7, /device:TPU:1, one launch (start us, length us, event | category | flops | bytes accessed | tf_op | source)
XLA Modules:
  0.0 59.9 jit_solution(213225721248554980)
XLA Ops:
  0.0 58.7 %shard_map.73 = f32[1,128]{1,0:T(1,128)} custom-call(bf16[576,128]{1,0:T(8,128)(2,1)} %bitcast.5, bf16[128,128]{1,0:T(8,128)(2,1)} %idx_hbm.1, bf16[128,4608]{1,0:T(8,128)(2,1)} %mq_hbm.1, bf16[128,512]{1,0:T(8,128)(2,1)} %iq_hbm.1, bf16[4,128]{1,0:T(4,128)(2,1)} %bitcast.7, s32[32,128]{1,0:T(8,128)} %bitcast.6, s32[1,64]{1,0:T(1,128)} %bitcast.8), custom_call_target="tpu_custom_call" | custom-call | tf_op jit(solution)/shard_map/pallas_call | solution.py:457
  58.7 1.2 %copy.9 = f32[128]{0:T(128)} copy(f32[128]{0:T(128)} %bitcast.9) | data formatting | bytes 1024

commit v8 on v6

--- a/solution.py
+++ b/solution.py
@@ -36,7 +36,7 @@
     lat_hbm, idx_hbm, mq_hbm, iq_hbm, gain_hbm, seg_hbm, order_hbm,
     out_ref,
     lat_in, idx_in, iq_in, gain_in, seg_in, order_in,
-    lat, mraw, mq, score, bias, iq_send, iq_recv, ilhs, iwide, ipack,
+    lat, mraw, mq, score, score_b, bias, iq_send, iq_recv, ilhs, iwide, ipack,
     slot_v, slot_s, tsend, trecv, town, kept, fsend, frecv,
     snd, rcv, xsend, xrecv, local, token,
 ):
@@ -319,7 +319,7 @@
         tail = jnp.where(lane // HALF == odd, tail, jnp.zeros_like(tail))
         return jnp.concatenate([main, tail], axis=1)
 
-    def scores_of(qb):
+    def scores_of(qb, score):
         def body(g, _):
             ks = jnp.concatenate([key_block(qb, g * GROUP + k) for k in range(GROUP)], axis=0)
             at = pl.ds(pl.multiple_of(g * GROUP * HALF, 256), GROUP * HALF)
@@ -334,7 +334,7 @@
         lane = lax.broadcasted_iota(jnp.int32, s.shape, 1)
         score[:, 0:128] = jnp.where((lane < HALF) & (lane <= row), s, score[:, 0:128])
 
-    def shares_of(qb):
+    def shares_of(qb, score):
         def slab(i, _):
             b = bias[qb, pl.ds(pl.multiple_of(i * 16, 16), 16), :]
             acc = jnp.zeros((16, width), F32)
@@ -399,9 +399,10 @@
     cross_step(far)
     sibling_wait()
 
-    for qb in (0, 1):
-        scores_of(qb)
-        shares_of(qb)
+    for qb, table in ((0, score), (1, score_b)):
+        scores_of(qb, table)
+    for qb, table in ((0, score), (1, score_b)):
+        shares_of(qb, table)
 
     index_scores()
     seen_bias = packed_bias()
@@ -469,6 +470,7 @@
             pltpu.VMEM((rows, heads * kdim), BF16),
             pltpu.VMEM((2, wide, LAT + 2 * ROPE), BF16),
             pltpu.VMEM((wide, width), F32),
+            pltpu.VMEM((wide, width), F32),
             pltpu.VMEM((2, HALF, width), F32),
             pltpu.VMEM((8, 16, iheads * 128 + 128), BF16),
             pltpu.VMEM((nh, 16, iheads * 128 + 128), BF16),

time: 59.5 us -> 60.2 us (1.012)
    pallas_call x1, Pallas kernels: 58.2 us -> 58.8 us  [per_device(): pl.pallas_call(functools.partial(fused, ny, nh, reach, heads, iheads), ou...]
where the time goes in v8:
time: 60.2 us; the launch traced here: 60 us
  Pallas kernels  58.8 us (98%)
  local copies, waits for them, and re-layouts  1.19 us (2%)
    pallas_call x1, Pallas kernels, per_device(): pl.pallas_call(functools.partial(fused, ny, nh, reach, heads, iheads), ou...  58.8 us

profile of v8, /device:TPU:1, one launch (start us, length us, event | category | flops | bytes accessed | tf_op | source)
XLA Modules:
  0.0 60.0 jit_solution(7383651913637123393)
XLA Ops:
  0.0 58.8 %shard_map.73 = f32[1,128]{1,0:T(1,128)} custom-call(bf16[576,128]{1,0:T(8,128)(2,1)} %bitcast.5, bf16[128,128]{1,0:T(8,128)(2,1)} %idx_hbm.1, bf16[128,4608]{1,0:T(8,128)(2,1)} %mq_hbm.1, bf16[128,512]{1,0:T(8,128)(2,1)} %iq_hbm.1, bf16[4,128]{1,0:T(4,128)(2,1)} %bitcast.7, s32[32,128]{1,0:T(8,128)} %bitcast.6, s32[1,64]{1,0:T(1,128)} %bitcast.8), custom_call_target="tpu_custom_call" | custom-call | tf_op jit(solution)/shard_map/pallas_call | solution.py:457
  58.8 1.2 %copy.9 = f32[128]{0:T(128)} copy(f32[128]{0:T(128)} %bitcast.9) | data formatting | bytes 1024
